TPU v7x, 512 devices: a whole 4x8x8 slice. The times are simulated.
512 devices in a mesh: row: 8 (over x, core), col: 16 (over y, z_lo), depth: 4 (over z_hi).
Axes of the slice: x: 4, y: 8, z: 8 (z_hi: 4, z_lo: 2; z = z_hi * 2 + z_lo), core: 2. Of those that a mesh axis runs over, the one named last changes fastest.
Arguments:
- upstream: float32 [49152, 1024], P(('row', 'col'), 'depth'), may hold values from -6 to 6
- preact: float32 [49152, 1024], P(('row', 'col'), 'depth'), may hold values from -6 to 6
- features: float32 [49152, 1024], P(('col', 'row'), 'depth'), may hold values from -0.02734375 to 0.02734375
- weight: float32 [1024, 1024], P('depth'), may hold values from -0.1875 to 0.1875
- blocks: float32 [8, 16, 32, 128, 128], P('row', 'col'), may hold values from -0.25 to 0.25
- block_pos: int32 [8, 16, 32], P('row', 'col'), may hold values from 0 to 1151, as said below
- block_count: int32 [8, 16], P('row', 'col'), may hold values from 1 to 32, as said below
Outputs:
- grad_features: float32 [49152, 1024], P(('col', 'row'), 'depth')
- grad_weight: float32 [1024, 1024], P(('depth', 'col'))
Inputs may be any that keep to these rules, and one draw needn't show every extreme that they name: `block_pos`: within one tile the positions are distinct. `block_count`: every tile of the first tile row has all 32 slots live; other tiles have at most 16.
All inputs are finite; a program needn't handle non-finite values.
Results may differ from a plain program's by a relative error of at most 0.0006.
Values sent between devices are 32-bit elements; how exact they have to be, the bound alone decides.
A program may use at most 64 MiB of HBM per device.

v0:
```python
import jax
import jax.numpy as jnp
from jax import lax
from jax.sharding import PartitionSpec as P

BLK = 128


def body(upstream, preact, features, weight, blocks, block_pos, block_count):
    signal = upstream * (preact > 0).astype(jnp.float32)
    width = signal.shape[1]
    local_rows = features.shape[0]
    tile_signal = lax.all_gather(signal, "col", axis=0, tiled=True)
    rows_per_block = tile_signal.shape[0] // BLK
    block_cols = local_rows * lax.axis_size("row") // BLK
    slot_count = blocks.shape[2]
    tiles = blocks.reshape(slot_count, BLK, BLK)
    where = block_pos.reshape(slot_count)
    count = block_count.reshape(())
    live = (jnp.arange(slot_count, dtype=jnp.int32) < count).astype(jnp.float32)
    picked = tile_signal.reshape(rows_per_block, BLK, width)[where // block_cols]
    contribution = jnp.einsum("kab,kaf->kbf", tiles, picked, precision=lax.Precision.HIGHEST)
    contribution = contribution * live[:, None, None]
    placement_choice = (
        (where % block_cols)[:, None] == jnp.arange(block_cols, dtype=jnp.int32)[None, :]
    ).astype(jnp.float32)
    partial_backward = jnp.einsum(
        "pa,pwh->awh", placement_choice, contribution, precision=lax.Precision.HIGHEST
    )
    partial_backward = partial_backward.reshape(block_cols * BLK, width)
    total = lax.psum(partial_backward, "row")
    mine = lax.dynamic_slice_in_dim(total, lax.axis_index("row") * local_rows, local_rows, 0)
    back_full = lax.all_gather(mine, "depth", axis=1, tiled=True)
    grad_features = jnp.einsum("ng,fg->nf", back_full, weight, precision=lax.Precision.HIGHEST)
    share = lax.psum_scatter(
        jnp.einsum("nf,ng->fg", features, back_full, precision=lax.Precision.HIGHEST),
        "col",
        scatter_dimension=0,
        tiled=True,
    )
    grad_weight = lax.psum(share, "row")
    return (grad_features, grad_weight)


def solution(mesh):
    in_specs = (
        P(("row", "col"), "depth"),
        P(("row", "col"), "depth"),
        P(("col", "row"), "depth"),
        P("depth", None),
        P("row", "col", None, None, None),
        P("row", "col", None),
        P("row", "col"),
    )
    out_specs = (P(("col", "row"), "depth"), P(("depth", "col"), None))
    return jax.shard_map(body, mesh=mesh, in_specs=in_specs, out_specs=out_specs, check_vma=False)
```

profile of v0, /device:TPU:1, one launch (start us, length us, event | category | flops | bytes accessed | tf_op | source)
XLA Modules:
  0.0 474.5 jit_solution(4736276273992523210)
XLA Ops:
  7.2 0.0 copy-start
  7.2 0.0 all-gather.3.cloned.1.call-start
  7.2 2.0 compare_select_fusion
  9.3 0.0 all-gather.3.cloned.1.call-update
  9.3 0.0 all-reduce.3.cloned.1.call-start
  10.0 0.7 fusion.5
  10.7 0.7 and_select_fusion
  11.4 148.1 %all-gather.3.cloned.1.call-done = f32[6144,256]{1,0:T(8,128)} async-done(((f32[384,256]{1,0:T(8,128)}), f32[6144,256]{1,0:T(8,128)}) %all-gather.3.cloned.1.call-update) | async-done | bytes 6291472 | tf_op jit(solution)/shard_map/all_gather | solution.py:13
  159.5 5.6 %gather_fusion = f32[32,128,256]{2,1,0:T(8,128)} fusion(f32[48,128,256]{2,1,0:T(8,128)} %bitcast.34, s32[1024]{0:T(1024)S(1)} %pad_clamp_fusion), kind=kCustom, calls=%fused_computation | custom fusion | bytes 8388736 | tf_op jit(solution)/shard_map/gather | solution.py:21
  165.1 0.0 copy-done
  165.1 10.7 %multiply_bitcast_fusion = f32[32,128,256]{1,2,0:T(8,128)} fusion(f32[32,128,256]{2,1,0:T(8,128)} %gather_fusion, f32[1,1,32,128,128]{4,3,2,1,0:T(8,128)S(1)} %copy-done, f32[32]{0:T(128)S(1)} %compare_convert_fusion), kind=kOutput, calls=%fused_computation.1 | convolution fusion | flops 1611661312 | bytes 10485888 | tf_op jit(solution)/shard_map/kab,kaf->kbf/dot_general | solution.py:22
  175.9 5.5 %copy.16 = f32[32,128,256]{2,0,1:T(8,128)} copy(f32[32,128,256]{1,2,0:T(8,128)} %multiply_bitcast_fusion) | data formatting | bytes 8388608 | tf_op jit(solution)/shard_map/mul | solution.py:23
  181.4 4.1 fusion.2
  185.4 0.0 copy-start.1
  185.5 2.7 copy.17
  188.1 0.0 all-reduce.3.cloned.1.call-update
  188.1 0.0 all-gather.5.cloned.1.call-start
  188.2 78.9 %all-reduce.3.cloned.1.call-done = f32[3072,256]{1,0:T(8,128)} async-done(((f32[3072,256]{1,0:T(8,128)}), f32[3072,256]{1,0:T(8,128)}) %all-reduce.3.cloned.1.call-update) | async-done | bytes 3145744 | tf_op jit(solution)/shard_map/psum | solution.py:31
  267.1 1.8 constant_dynamic-slice_fusion
  268.9 0.0 all-gather.5.cloned.1.call-update
  268.9 0.0 reduce-scatter.4.cloned.1.call-start
  268.9 49.0 %all-gather.5.cloned.1.call-done = f32[384,1024]{1,0:T(8,128)} async-done(((f32[384,256]{1,0:T(8,128)}), f32[384,1024]{1,0:T(8,128)}) %all-gather.5.cloned.1.call-update) | async-done | bytes 1572880 | tf_op jit(solution)/shard_map/all_gather | solution.py:33
  317.9 0.0 copy-done.1
  317.9 4.0 convolution_bitcast_fusion
  322.0 1.3 copy.20
  323.3 0.0 reduce-scatter.4.cloned.1.call-update
  323.3 0.0 all-reduce.5.cloned.1.call-start
  323.4 61.1 %reduce-scatter.4.cloned.1.call-done = f32[16,1024]{1,0:T(8,128)} async-done(((f32[256,1024]{1,0:T(8,128)}), f32[16,1024]{1,0:T(8,128)}) %reduce-scatter.4.cloned.1.call-update) | async-done | bytes 65552
  384.5 1.8 copy.21
  386.3 0.0 all-reduce.5.cloned.1.call-update
  386.4 3.9 fusion.6
  390.2 75.8 %all-reduce.5.cloned.1.call-done = f32[16,1024]{0,1:T(8,128)} async-done(((f32[16,1024]{0,1:T(8,128)}), f32[16,1024]{0,1:T(8,128)}) %all-reduce.5.cloned.1.call-update) | async-done | bytes 65552 | tf_op jit(solution)/shard_map/psum | solution.py:41
  466.1 1.8 copy.18
  (2 shorter events, 0.0 us)
Async XLA Ops:
  7.2 158.0 %copy-start = (f32[1,1,32,128,128]{4,3,2,1,0:T(8,128)S(1)}, f32[1,1,32,128,128]{4,3,2,1,0:T(8,128)}, u32[]{:S(2)}) copy-start(f32[1,1,32,128,128]{4,3,2,1,0:T(8,128)} %param.11) | copy-start | bytes 6291460
  7.2 152.3 %all-gather.3.cloned.1.call-start = ((), (), s32[]{:S(2)}) async-start(), calls=%async_computation.1 | async-start | bytes 6684672 | tf_op jit(solution)/shard_map/all_gather | solution.py:13
  9.3 257.8 %all-reduce.3.cloned.1.call-start = ((), (), s32[]{:S(2)}) async-start(), calls=%async_computation.2 | async-start | bytes 6291456 | tf_op jit(solution)/shard_map/psum | solution.py:31
  185.4 132.5 %copy-start.1 = (f32[384,256]{1,0:T(8,128)S(1)}, f32[384,256]{1,0:T(8,128)}, u32[]{:S(2)}) copy-start(f32[384,256]{1,0:T(8,128)} %param.9) | copy-start | bytes 1179652
  188.1 129.8 %all-gather.5.cloned.1.call-start = ((), (), s32[]{:S(2)}) async-start(), calls=%async_computation.3 | async-start | bytes 1966080 | tf_op jit(solution)/shard_map/all_gather | solution.py:33
  268.9 115.6 %reduce-scatter.4.cloned.1.call-start = ((), (), s32[]{:S(2)}) async-start(), calls=%async_computation.5 | async-start | bytes 1114112
  323.3 142.8 %all-reduce.5.cloned.1.call-start = ((), (), s32[]{:S(2)}) async-start(), calls=%async_computation.4 | async-start | bytes 1048576 | tf_op jit(solution)/shard_map/psum | solution.py:41
Sparse Core Ops, SparseCore 0:
  10.7 148.7 all-gather.2
  188.3 78.7 all-reduce.2
  269.8 48.1 all-gather.4
  323.5 61.0 reduce-scatter.3
  386.8 79.2 all-reduce.4
where the time goes:
time: 475 us; the launch traced here: 474 us
  waiting for transfers between devices  413 us (87%)
  matrix products  22.7 us (5%)
  local copies, waits for them, and re-layouts  20.5 us (4%)
  between operations  14.5 us (3%)
    all_gather x1, waiting for transfers between devices, body(): tile_signal = lax.all_gather(signal, 'col', axis=0, tiled=True)  148 us
    psum x1, waiting for transfers between devices, body(): total = lax.psum(partial_backward, 'row')  78.9 us
    psum x1, waiting for transfers between devices, body(): grad_weight = lax.psum(share, 'row')  75.8 us
    unnamed x6, waiting for transfers between devices  61.2 us
    all_gather x1, waiting for transfers between devices, body(): back_full = lax.all_gather(mine, 'depth', axis=1, tiled=True)  49 us
    dot_general x1, matrix products, body(): jnp.einsum('kab,kaf->kbf', tiles, picked, precision=lax.Precision.HIGHEST)  10.7 us
  transfers between devices with their start and end apart: 5, of which 5 were waited for; matrix products, arithmetic and copies ran while one was open for 1% of the time, Pallas kernels for 0%

commit v1 on v0

v1 whole, which is shorter than its diff:
```python
import functools

import jax
import jax.numpy as jnp
from jax import lax
from jax.experimental import pallas as pl
from jax.experimental.pallas import tpu as pltpu
from jax.sharding import PartitionSpec as P

BLK = 128
Q = 2
F = 128 // Q
MESH = pl.DeviceIdType.MESH
F32 = jnp.float32
BF16 = jnp.bfloat16
NT = (((1,), (1,)), ((), ()))


def split(v):
    hi = v.astype(BF16)
    return hi, (v - hi.astype(F32)).astype(BF16)


def dot(a, b):
    return jnp.dot(a, b, preferred_element_type=F32)


def dot_nt(a, b):
    return lax.dot_general(a, b, NT, preferred_element_type=F32)


def dot3(ah, al, bh, bl, f):
    return f(ah, bh) + f(al, bh) + f(ah, bl)


def kernel(up, pre, tab_v, tab_own, feat_hbm, w_hbm, blk_hbm, gf_out, gw_out,
           turned, peer_tab_v, peer_tab, own_blk, peer_blk, blk_hi, blk_lo, run,
           feat, wv, ft_hi, ft_lo, w_hi, w_lo, gft,
           gw, gw_in, gw_half, gw_yz, gw_fin, *rest):
    sig = rest[:Q]
    part = rest[Q:2 * Q]
    core_in = rest[2 * Q:3 * Q]
    far_in = rest[3 * Q:4 * Q]
    near_in = rest[4 * Q:5 * Q]
    back = rest[5 * Q:6 * Q]
    other = rest[6 * Q:7 * Q]
    (loc, swap_s, swap_r, tab_s, tab_r, blk_s, blk_r, y_s, y_r, core_s, core_r,
     far_s, far_r, near_s, near_r, z_s, z_r, gwr_s, gwr_r, gwy_s, gwy_r, gwf_s, gwf_r) = rest[7 * Q:]

    r = lax.axis_index("row")
    c = lax.axis_index("col")
    zh = lax.axis_index("depth")
    x, k = r // 2, r % 2
    y, zl = c // 2, c % 2
    z = zh * 2 + zl

    def at(dx=0, dk=0, dy=0, dz=0):
        zz = (z + dz + 8) % 8
        return {"row": ((x + dx + 4) % 4) * 2 + (k + dk) % 2,
                "col": ((y + dy + 8) % 8) * 2 + zz % 2, "depth": zz // 2}

    peer = {"row": r, "col": y * 2 + 1 - zl, "depth": zh}
    pending = []

    def copy(src, dst, ssem, rsem, dev):
        return pltpu.make_async_remote_copy(src_ref=src, dst_ref=dst, send_sem=ssem, recv_sem=rsem,
                                            device_id=dev, device_id_type=MESH)

    def send(src, dst, ssem, rsem, dev):
        cp = copy(src, dst, ssem, rsem, dev)
        cp.start()
        pending.append(cp)

    def got(dst, ssem, rsem):
        copy(dst, dst, ssem, rsem, peer).wait_recv()

    bar = pltpu.get_barrier_semaphore()

    def greet(dev):
        pl.semaphore_signal(bar, inc=1, device_id=dev, device_id_type=MESH)

    @pl.loop(1, 8)
    def _(j):
        greet({"row": (r + j) % 8, "col": c, "depth": zh})

    @pl.loop(1, 16)
    def _(j):
        greet({"row": r, "col": (c + j) % 16, "depth": zh})

    out_dz = jnp.where(zl == 0, -1, 1)
    greet(at(dz=out_dz))
    greet(at(dz=2))
    greet(at(dz=-2))

    local = [pltpu.make_async_copy(s, d, loc.at[i]) for i, (s, d) in enumerate(
        ((blk_hbm, own_blk), (feat_hbm, feat), (w_hbm, wv)))]
    for cp in local:
        cp.start()

    for i in range(3):
        for h in range(2):
            u = up[i * BLK:(i + 1) * BLK, h * BLK:(h + 1) * BLK]
            p = pre[i * BLK:(i + 1) * BLK, h * BLK:(h + 1) * BLK]
            turned[h, i] = (u * (p > 0).astype(F32)).T
    for i in range(3):
        v = turned[zl, i]
        for q in range(Q):
            sig[q][6 * y + 3 * zl + i] = v[q * F:(q + 1) * F]

    pl.semaphore_wait(bar, 25)

    n_slots = jnp.where(r == 0, 32, 16)

    def swap_send(q):
        send(turned.at[1 - zl, :, pl.ds(q * F, F)], sig[q].at[pl.ds(6 * y + 3 * zl, 3)],
             swap_s.at[q], swap_r.at[q], peer)

    def swap_wait(q):
        got(sig[q].at[pl.ds(6 * y + 3 * (1 - zl), 3)], swap_s.at[q], swap_r.at[q])

    def y_piece(q, yo, hr):
        h = zl if hr == 0 else 1 - zl
        return sig[q].at[pl.ds(6 * yo + 3 * h, 3)]

    def y_send(q, d, s, hr):
        sgn = 1 - 2 * d
        ref = y_piece(q, (y - sgn * (s - 1) + 8) % 8, hr)
        send(ref, ref, y_s.at[q, d, hr, s - 1], y_r.at[q, d, hr, s - 1], at(dy=sgn))

    def y_first(q, hr):
        for d in range(2):
            y_send(q, d, 1, hr)

    def y_step(q, s, hr):
        for d in range(2):
            last = 4 if d == hr else 3
            if s > last:
                continue
            sgn = 1 - 2 * d
            got(y_piece(q, (y - sgn * s + 8) % 8, hr), y_s.at[q, d, hr, s - 1], y_r.at[q, d, hr, s - 1])
            if s < last:
                y_send(q, d, s + 1, hr)

    def blk_copy(j):
        lo = 8 * j
        return copy(blk_hbm.at[pl.ds(lo, 8)], peer_blk.at[pl.ds(lo, 8)], blk_s.at[j], blk_r.at[j],
                    at(dz=1 if j % 2 == 0 else -1))

    def blk_send():
        send(tab_v, peer_tab_v, tab_s.at[0], tab_r.at[0], peer)
        for j in range(2):
            blk_copy(j).start()

        @pl.when(r == 0)
        def _():
            for j in range(2, 4):
                blk_copy(j).start()

    def blk_wait():
        for j in range(2):
            blk_copy(j).wait_recv()

        @pl.when(r == 0)
        def _():
            for j in range(2, 4):
                blk_copy(j).wait_recv()

    def blk_done():
        for j in range(2):
            blk_copy(j).wait_send()

        @pl.when(r == 0)
        def _():
            for j in range(2, 4):
                blk_copy(j).wait_send()

    def split_blocks(rel):
        src = own_blk if rel == 0 else peer_blk

        @pl.loop(0, n_slots)
        def _(i):
            hi, lo = split(src[i])
            blk_hi[rel, i] = hi
            blk_lo[rel, i] = lo

    def prep_own():
        local[0].wait()
        split_blocks(0)

    def prep_peer():
        got(peer_tab_v, tab_s.at[0], tab_r.at[0])
        cp = pltpu.make_async_copy(peer_tab_v, peer_tab, loc.at[3])
        cp.start()
        blk_wait()
        split_blocks(1)
        cp.wait()

    def prep_feat():
        local[1].wait()
        for i in range(3):
            for h in range(2):
                t = feat[i * BLK:(i + 1) * BLK, h * BLK:(h + 1) * BLK].T
                t = t.reshape(8, 2, 8, BLK)
                for kk in range(2):
                    hi, lo = split(t[:, kk].reshape(64, BLK))
                    row = kk * BLK + h * 64
                    ft_hi[row:row + 64, i * BLK:(i + 1) * BLK] = hi
                    ft_lo[row:row + 64, i * BLK:(i + 1) * BLK] = lo

    def prep_w():
        local[2].wait()
        for q in range(Q):
            v = jnp.concatenate([wv[:, zz * BLK + q * F:zz * BLK + (q + 1) * F] for zz in range(8)], axis=1)
            w_hi[q], w_lo[q] = split(v)

    def spmm(q, rel):
        tab = tab_own if rel == 0 else peer_tab

        def body(it, acc):
            terms = []
            for u in range(4):
                i = it * 4 + u
                sh, sl = split(sig[q][tab[0, i]])
                o = tab[1, i]
                bh, bl = blk_hi[rel, o], blk_lo[rel, o]
                terms.append(dot3(sh, sl, bh, bl, dot) * tab[2, i].astype(F32))
            for u in range(4):
                i = it * 4 + u
                acc = terms[u] + acc * tab[3, i].astype(F32)
                run[i] = acc
            return acc

        lax.fori_loop(0, n_slots // 4, body, jnp.zeros((F, BLK), F32))
        for b in range(24):
            rr = b // 3
            part[q][rr // 2, rr % 2, rel, b % 3] = run[tab[4, b]] * tab[5, b].astype(F32)

    def core_send(q):
        for o in (2, 1, 3, 0):
            xx = (x + o) % 4
            send(part[q].at[xx, 1 - k], core_in[q].at[xx], core_s.at[q, o], core_r.at[q, o], at(dk=1))

    def core_sum(q, o):
        xx = (x + o) % 4
        got(core_in[q].at[xx], core_s.at[q, o], core_r.at[q, o])
        part[q][xx, k] = part[q][xx, k] + core_in[q][xx]

    def x_far(q):
        core_sum(q, 2)
        xx = (x + 2) % 4
        for rel, sgn in ((0, 1), (1, -1)):
            send(part[q].at[xx, k, rel], far_in[q].at[rel], far_s.at[q, rel], far_r.at[q, rel], at(dx=sgn))

    def x_near(q):
        for rel, sgn in ((0, 1), (1, -1)):
            o = sgn % 4
            core_sum(q, o)
            xx = (x + o) % 4
            got(far_in[q].at[rel], far_s.at[q, rel], far_r.at[q, rel])
            part[q][xx, k, rel] = part[q][xx, k, rel] + far_in[q][rel]
            send(part[q].at[xx, k], near_in[q].at[rel], near_s.at[q, rel], near_r.at[q, rel], at(dx=sgn))
        core_sum(q, 0)

    def z_piece(q, dz):
        return back[q].at[pl.ds(((z + dz + 8) % 8) * F, F)]

    def z_start(q):
        for rel in range(2):
            got(near_in[q].at[rel], near_s.at[q, rel], near_r.at[q, rel])
        for rel in range(2):
            for i in range(3):
                v = part[q][x, k, rel, i] + near_in[q][0, rel, i] + near_in[q][1, rel, i]
                if rel == 0:
                    back[q][pl.ds(z * F, F), i * BLK:(i + 1) * BLK] = v
                else:
                    other[q][:, i * BLK:(i + 1) * BLK] = v
        for d, sgn in ((0, 1), (1, -1)):
            send(other[q], z_piece(q, 0), z_s.at[q, d], z_r.at[q, d], at(dz=sgn))
        for d, sgn in ((0, 1), (1, -1)):
            send(z_piece(q, 0), z_piece(q, 0), z_s.at[q, 2 + d], z_r.at[q, 2 + d], at(dz=2 * sgn))

    def z_near(q):
        for d, sgn in ((0, 1), (1, -1)):
            ref = z_piece(q, -sgn)
            got(ref, z_s.at[q, d], z_r.at[q, d])
            send(ref, ref, z_s.at[q, 4 + d], z_r.at[q, 4 + d], at(dz=2 * sgn))

    def z_half(q, dz, d):
        return back[q].at[pl.ds(((z + dz + 8) % 8) * F + d * (F // 2), F // 2)]

    def z_two(q):
        for d, sgn in ((0, 1), (1, -1)):
            got(z_piece(q, -2 * sgn), z_s.at[q, 2 + d], z_r.at[q, 2 + d])
            ref = z_half(q, -2 * sgn, d)
            send(ref, ref, z_s.at[q, 6 + d], z_r.at[q, 6 + d], at(dz=2 * sgn))

    def z_end(q):
        for d, sgn in ((0, 1), (1, -1)):
            got(z_piece(q, -3 * sgn), z_s.at[q, 4 + d], z_r.at[q, 4 + d])
        for d, sgn in ((0, 1), (1, -1)):
            got(z_half(q, -4 * sgn, d), z_s.at[q, 6 + d], z_r.at[q, 6 + d])

    def gemm(q):
        bh, bl = split(back[q][...])
        g = dot3(ft_hi[...], ft_lo[...], bh, bl, dot_nt)
        for xx in range(4):
            gw[q, xx] = g[:, xx * BLK:(xx + 1) * BLK].reshape(2, BLK, BLK)
        gw_send(q)
        t = dot3(w_hi[q], w_lo[q], bh, bl, dot)
        if q == 0:
            gft[...] = t
        elif q < Q - 1:
            gft[...] = gft[...] + t
        else:
            t = gft[...] + t
            for i in range(3):
                for h in range(2):
                    gf_out[i * BLK:(i + 1) * BLK, h * BLK:(h + 1) * BLK] = (
                        t[h * BLK:(h + 1) * BLK, i * BLK:(i + 1) * BLK].T)

    def gw_row(q, j):
        rr = (r + j) % 8
        return copy(gw.at[q, rr // 2, rr % 2], gw_in.at[q, j], gwr_s.at[q, j], gwr_r.at[q, j],
                    {"row": rr, "col": c, "depth": zh})

    def gw_col(q, j):
        cc = (c + j) % 16
        return copy(gw_half.at[q, cc], gw_yz.at[q, j], gwy_s.at[q, j], gwy_r.at[q, j],
                    {"row": r, "col": cc, "depth": zh})

    def gw_all(q, j):
        rr = (r + j) % 8
        return copy(gw_fin.at[q, r], gw_fin.at[q, r], gwf_s.at[q, j], gwf_r.at[q, j],
                    {"row": rr, "col": c, "depth": zh})

    def gw_all_in(q, j):
        ref = gw_fin.at[q, (r - j + 8) % 8]
        return copy(ref, ref, gwf_s.at[q, j], gwf_r.at[q, j], peer)

    def gw_send(q):
        @pl.loop(1, 8)
        def _(j):
            gw_row(q, j).start()

    def gw_sum(q):
        @pl.loop(1, 8)
        def _(j):
            gw_row(q, j).wait_recv()
        v = gw[q, x, k]
        for j in range(1, 8):
            v = v + gw_in[q, j]
        gw_half[q] = v.reshape(16, 8, BLK)

        @pl.loop(1, 16)
        def _(j):
            gw_col(q, j).start()

    def gw_cols(q):
        @pl.loop(1, 16)
        def _(j):
            gw_col(q, j).wait_recv()
        v = gw_half[q, c]
        for j in range(1, 16):
            v = v + gw_yz[q, j]
        gw_fin[q, r] = v

        @pl.loop(1, 8)
        def _(j):
            gw_all(q, j).start()

    def gw_end():
        for q in range(Q):
            @pl.loop(1, 8)
            def _(j):
                gw_all_in(q, j).wait_recv()
        for xx in range(4):
            for kk in range(2):
                for zz in range(2):
                    v = jnp.concatenate([gw_fin[q, 2 * xx + kk][:, zz * F:(zz + 1) * F] for q in range(Q)], axis=1)
                    lane = (2 * xx + zz) * BLK
                    gw_out[kk * 8:(kk + 1) * 8, lane:lane + BLK] = v

    def drain():
        for cp in pending:
            cp.wait_send()
        blk_done()
        for q in range(Q):
            @pl.loop(1, 8)
            def _(j):
                gw_row(q, j).wait_send()
                gw_all(q, j).wait_send()

            @pl.loop(1, 16)
            def _(j):
                gw_col(q, j).wait_send()

    def tail(q):
        return [(spmm, q, 0), (spmm, q, 1), (core_send, q), (x_far, q), (x_near, q),
                (z_start, q), (z_near, q), (z_two, q), (z_end, q), (gemm, q), (gw_sum, q), (gw_cols, q)]

    order = [
        (swap_send, 0), (y_first, 0, 0), (swap_send, 1), (blk_send,), (swap_wait, 0), (y_first, 0, 1),
        (prep_feat,), (y_step, 0, 1, 0), (y_step, 0, 1, 1), (prep_w,), (y_step, 0, 2, 0), (y_step, 0, 2, 1),
        (prep_own,), (y_step, 0, 3, 0), (swap_wait, 1), (y_first, 1, 0), (y_step, 0, 3, 1), (y_first, 1, 1),
        (y_step, 0, 4, 0), (y_step, 0, 4, 1), (prep_peer,),
        (spmm, 0, 0), (y_step, 1, 1, 0), (spmm, 0, 1), (core_send, 0), (y_step, 1, 1, 1), (y_step, 1, 2, 0),
        (x_far, 0), (y_step, 1, 2, 1), (y_step, 1, 3, 0), (x_near, 0), (y_step, 1, 3, 1),
        (y_step, 1, 4, 0), (y_step, 1, 4, 1),
        (spmm, 1, 0), (spmm, 1, 1), (core_send, 1), (z_start, 0),
        (x_far, 1), (z_near, 0), (x_near, 1), (z_two, 0), (z_start, 1), (z_end, 0),
        (gemm, 0), (z_near, 1), (z_two, 1), (gw_sum, 0), (gw_cols, 0), (z_end, 1), (gemm, 1), (gw_sum, 1),
        (gw_cols, 1), (gw_end,), (drain,),
    ]
    for fn, *args in order:
        fn(*args)


def tables(block_pos, block_count):
    n = block_pos.shape[-1]
    pos = block_pos.reshape(n)
    i = jnp.arange(n, dtype=jnp.int32)
    live = (i < block_count.reshape(())).astype(jnp.int32)
    col = jnp.where(live == 1, pos % 24, 24)
    key = col * n + i
    rank = jnp.sum((key[None, :] < key[:, None]).astype(jnp.int32), axis=1)
    hot = (rank[None, :] == i[:, None]).astype(jnp.int32)
    row_s = jnp.sum(hot * (pos // 24)[None, :], axis=1)
    slot_s = jnp.sum(hot * i[None, :], axis=1)
    live_s = jnp.sum(hot * live[None, :], axis=1)
    same = (col[None, :] == col[:, None]).astype(jnp.int32)
    seen = jnp.sum(same * (i[None, :] < i[:, None]).astype(jnp.int32), axis=1)
    cont = jnp.sum(hot * ((seen > 0) & (live == 1)).astype(jnp.int32)[None, :], axis=1)
    b = jnp.arange(24, dtype=jnp.int32)
    at_col = (col[None, :] == b[:, None]).astype(jnp.int32)
    last = jnp.max(at_col * rank[None, :], axis=1)
    has = jnp.max(at_col, axis=1)

    def line(v):
        return jnp.pad(v, (0, BLK - v.shape[0]))[None]

    zero = jnp.zeros((2, BLK), jnp.int32)
    return jnp.concatenate([line(row_s), line(slot_s), line(live_s), line(cont), line(last), line(has), zero])


def body(upstream, preact, features, weight, blocks, block_pos, block_count):
    tab = tables(block_pos, block_count)
    vmem = pl.BlockSpec(memory_space=pltpu.VMEM)
    smem = pl.BlockSpec(memory_space=pltpu.SMEM)
    hbm = pl.BlockSpec(memory_space=pl.ANY)
    dma = pltpu.SemaphoreType.DMA
    V = pltpu.VMEM
    scratch = [
        V((2, 3, BLK, BLK), F32),
        V((8, BLK), jnp.int32),
        pltpu.SMEM((8, BLK), jnp.int32),
        V((32, BLK, BLK), F32), V((32, BLK, BLK), F32),
        V((2, 32, BLK, BLK), BF16), V((2, 32, BLK, BLK), BF16),
        V((32, F, BLK), F32),
        V((384, 256), F32), V((256, 1024), F32),
        V((256, 384), BF16), V((256, 384), BF16),
        V((Q, 256, 8 * F), BF16), V((Q, 256, 8 * F), BF16),
        V((256, 384), F32),
        V((Q, 4, 2, BLK, BLK), F32),
        V((Q, 8, BLK, BLK), F32),
        V((Q, 16, 8, BLK), F32),
        V((Q, 16, 8, BLK), F32),
        V((Q, 8, 8, BLK), F32),
    ]
    for shape in ((48, F, BLK), (4, 2, 2, 3, F, BLK), (4, 2, 3, F, BLK), (2, 3, F, BLK),
                  (2, 2, 3, F, BLK), (8 * F, 384), (F, 384)):
        scratch += [V(shape, F32) for _ in range(Q)]
    scratch += [
        dma((4,)), dma((Q,)), dma((Q,)), dma((1,)), dma((1,)), dma((4,)), dma((4,)),
        dma((Q, 2, 2, 4)), dma((Q, 2, 2, 4)), dma((Q, 4)), dma((Q, 4)),
        dma((Q, 2)), dma((Q, 2)), dma((Q, 2)), dma((Q, 2)), dma((Q, 8)), dma((Q, 8)),
        dma((Q, 8)), dma((Q, 8)), dma((Q, 16)), dma((Q, 16)), dma((Q, 8)), dma((Q, 8)),
    ]
    return pl.pallas_call(
        kernel,
        out_shape=(jax.ShapeDtypeStruct((384, 256), F32), jax.ShapeDtypeStruct((16, 1024), F32)),
        in_specs=[vmem, vmem, vmem, smem, hbm, hbm, hbm],
        out_specs=(vmem, vmem),
        scratch_shapes=scratch,
        compiler_params=pltpu.CompilerParams(
            collective_id=0, has_side_effects=True, vmem_limit_bytes=56 * 2**20),
        cost_estimate=pl.CostEstimate(flops=2 * 10**9, bytes_accessed=6 * 2**20, transcendentals=0),
        name="graph_backward",
    )(upstream, preact, tab, tab, features, weight, blocks.reshape(blocks.shape[2:]))


def solution(mesh):
    in_specs = (
        P(("row", "col"), "depth"),
        P(("row", "col"), "depth"),
        P(("col", "row"), "depth"),
        P("depth", None),
        P("row", "col", None, None, None),
        P("row", "col", None),
        P("row", "col"),
    )
    out_specs = (P(("col", "row"), "depth"), P(("depth", "col"), None))
    return jax.shard_map(body, mesh=mesh, in_specs=in_specs, out_specs=out_specs, check_vma=False)
```

time: 475 us -> 115 us (0.24)
  waiting for transfers between devices: 413 us -> 0 us
  Pallas kernels: 0 us -> 109 us
  matrix products: 22.7 us -> 0 us
  local copies, waits for them, and re-layouts: 20.5 us -> 3.87 us
  between operations: 14.5 us -> 1.34 us
    all_gather x2 -> x0, waiting for transfers between devices: 197 us -> none  [the longest x1 148 us: body(): tile_signal = lax.all_gather(signal, 'col', axis=0, tiled=True)]
    psum x2 -> x0, waiting for transfers between devices: 155 us -> none  [the longest x1 78.9 us: body(): total = lax.psum(partial_backward, 'row')]
    pallas_call x0 -> x1, Pallas kernels: none -> 109 us  [body(): pl.pallas_call(kernel, out_shape=(jax.ShapeDtypeStruct((384, 256), F32),...]
    unnamed x6 -> x0, waiting for transfers between devices: 61.2 us -> none
    dot_general x4 -> x0, matrix products: 22.7 us -> none  [the longest x1 10.7 us: body(): jnp.einsum('kab,kaf->kbf', tiles, picked, precision=lax.Precision.HIGHEST)]
    gather x1 -> x0, local copies, waits for them, and re-layouts: 5.63 us -> none  [body(): tile_signal.reshape(rows_per_block, BLK, width)[where // block_cols]]
    mul x1 -> x0, local copies, waits for them, and re-layouts: 5.49 us -> none  [body(): contribution = contribution * live[:, None, None]]
  transfers between devices with their start and end apart: 5 -> 0, of which waited for: 5 -> 0; matrix products, arithmetic and copies ran while one was open for 1% -> 0% of each run, Pallas kernels for 0% -> 0%
where the time goes in v1:
time: 115 us
  Pallas kernels  109 us (95%)
  local copies, waits for them, and re-layouts  3.87 us (3%)
  between operations  1.34 us (1%)
  other arithmetic  1.3 us (1%)
    pallas_call x1, Pallas kernels, body(): pl.pallas_call(kernel, out_shape=(jax.ShapeDtypeStruct((384, 256), F32),...  109 us
    unnamed x2, local copies, waits for them, and re-layouts  3.24 us

profile of v1, /device:TPU:1, one launch (start us, length us, event | category | flops | bytes accessed | tf_op | source)
XLA Modules:
  0.0 115.0 jit_solution(5699560319950151725)
XLA Ops:
  1.3 0.7 iota_add_fusion
  1.9 0.2 convert_reduce_fusion
  2.1 0.2 select_reduce_fusion.1
  2.3 0.1 select_reduce_fusion
  2.5 0.1 convert_reduce_fusion.1
  2.7 0.6 concatenate.3.tab_v.tab_own
  3.3 108.5 %graph_backward.1 = (f32[384,256]{1,0:T(8,128)}, f32[16,1024]{1,0:T(8,128)}) custom-call(f32[384,256]{1,0:T(8,128)} %up.1, f32[384,256]{1,0:T(8,128)} %pre.1, s32[8,128]{1,0:T(8,128)} %concatenate.3.tab_v.tab_own, s32[8,128]{1,0:T(8,128)} %concatenate.3.tab_v.tab_own, f32[384,256]{1,0:T(8,128)} %feat_hbm.1, f32[256,1024]{1,0:T(8,128)} %w_hbm.1, ...), custom_call_target="tpu_custom_call" | custom-call | flops 2000000000 | bytes 6291456 | tf_op jit(solution)/shard_map/graph_backward/pallas_call | solution.py:478
  111.8 1.8 %copy.12 = f32[384,256]{1,0:T(8,128)} copy(f32[384,256]{1,0:T(8,128)} %get-tuple-element.17) | data formatting | bytes 786432
  113.5 1.5 %copy.13 = f32[16,1024]{1,0:T(8,128)} copy(f32[16,1024]{1,0:T(8,128)} %get-tuple-element.18) | data formatting | bytes 131072
  (7 shorter events, 0.0 us)

commit v2 on v1

v2 whole, which is shorter than its diff:
```python
import jax
import jax.numpy as jnp
from jax import lax
from jax.experimental import pallas as pl
from jax.experimental.pallas import tpu as pltpu
from jax.sharding import PartitionSpec as P

BLK = 128
CHUNKS = (64, 64)
Q = len(CHUNKS)
START = tuple(sum(CHUNKS[:q]) for q in range(Q))
MESH = pl.DeviceIdType.MESH
F32 = jnp.float32
BF16 = jnp.bfloat16
NT = (((1,), (1,)), ((), ()))


def split(v):
    hi = v.astype(BF16)
    return hi, (v - hi.astype(F32)).astype(BF16)


def dot(a, b):
    return jnp.dot(a, b, preferred_element_type=F32)


def dot_nt(a, b):
    return lax.dot_general(a, b, NT, preferred_element_type=F32)


def dot3(ah, al, bh, bl, f):
    return f(ah, bh) + f(al, bh) + f(ah, bl)


def down(row):
    return jnp.broadcast_to(row, (BLK, BLK)).T


def tables(pos, count):
    lane = lax.broadcasted_iota(jnp.int32, (1, BLK), 1)
    ii = lax.broadcasted_iota(jnp.int32, (BLK, BLK), 0)
    jj = lax.broadcasted_iota(jnp.int32, (BLK, BLK), 1)
    live = (lane < count).astype(jnp.int32)
    brow = (pos * 2731) >> 16
    col = jnp.where(live > 0, pos - 24 * brow, 24)
    col_i = down(col)
    key = col * BLK + lane
    rank = jnp.sum((down(key) < key).astype(jnp.int32), axis=0, keepdims=True)
    same = (col_i == col).astype(jnp.int32)
    seen = jnp.sum(same * (ii < jj).astype(jnp.int32), axis=0, keepdims=True)
    more = jnp.sum(same * (ii > jj).astype(jnp.int32), axis=0, keepdims=True)
    cont = jnp.where(seen > 0, live, 0)
    rank_i = down(rank)
    hot = (rank_i == jj).astype(jnp.int32)

    def put(v):
        return jnp.sum(hot * v, axis=0, keepdims=True)

    at_col = (col_i == jj).astype(jnp.int32)
    last = jnp.sum(at_col * down(jnp.where(more > 0, 0, rank)), axis=0, keepdims=True)
    has = (jnp.sum(at_col, axis=0, keepdims=True) > 0).astype(jnp.int32)
    return [put(down(brow)), put(ii), put(down(live)), put(down(cont)), last, has]


def kernel(up, pre, pos, count, feat_hbm, w_hbm, blk_hbm, gf_out, gw_out,
           turned, tab_v, tab_own, peer_tab_v, peer_tab, own_blk, peer_blk, blk_hi, blk_lo, run,
           feat, wv, ft_hi, ft_lo, gft, *rest):
    parts = [rest[i * Q:(i + 1) * Q] for i in range(16)]
    (sig, part, core_in, far_in, near_in, back, other, back_hi, back_lo, w_hi, w_lo,
     gw, gw_in, gw_half, gw_yz, gw_fin) = parts
    (loc, swap_s, swap_r, tab_s, tab_r, blk_s, blk_r, y_s, y_r, core_s, core_r,
     far_s, far_r, near_s, near_r, z_s, z_r, gwr_s, gwr_r, gwy_s, gwy_r, gwf_s, gwf_r) = rest[16 * Q:]

    r = lax.axis_index("row")
    c = lax.axis_index("col")
    zh = lax.axis_index("depth")
    x, k = r // 2, r % 2
    y, zl = c // 2, c % 2
    z = zh * 2 + zl

    def at(dx=0, dk=0, dy=0, dz=0):
        zz = (z + dz + 8) % 8
        return {"row": ((x + dx + 4) % 4) * 2 + (k + dk) % 2,
                "col": ((y + dy + 8) % 8) * 2 + zz % 2, "depth": zz // 2}

    peer = {"row": r, "col": y * 2 + 1 - zl, "depth": zh}
    pending = []

    def copy(src, dst, ssem, rsem, dev):
        return pltpu.make_async_remote_copy(src_ref=src, dst_ref=dst, send_sem=ssem, recv_sem=rsem,
                                            device_id=dev, device_id_type=MESH)

    def send(src, dst, ssem, rsem, dev):
        cp = copy(src, dst, ssem, rsem, dev)
        cp.start()
        pending.append(cp)

    def got(dst, ssem, rsem):
        copy(dst, dst, ssem, rsem, peer).wait_recv()

    bar = pltpu.get_barrier_semaphore()
    for dev in (at(dx=1), at(dx=-1), at(dk=1), at(dy=1), at(dy=-1), at(dz=1), at(dz=-1), at(dz=2), at(dz=-2)):
        pl.semaphore_signal(bar, inc=1, device_id=dev, device_id_type=MESH)

    local = [pltpu.make_async_copy(s, d, loc.at[i]) for i, (s, d) in enumerate(
        ((blk_hbm, own_blk), (feat_hbm, feat), (w_hbm, wv)))]
    for cp in local:
        cp.start()

    for i in range(3):
        for h in range(2):
            u = up[i * BLK:(i + 1) * BLK, h * BLK:(h + 1) * BLK]
            p = pre[i * BLK:(i + 1) * BLK, h * BLK:(h + 1) * BLK]
            turned[h, i] = (u * (p > 0).astype(F32)).T
    for i in range(3):
        v = turned[zl, i]
        for q in range(Q):
            sig[q][6 * y + 3 * zl + i] = v[START[q]:START[q] + CHUNKS[q]]

    pl.semaphore_wait(bar, 9)

    n_slots = jnp.where(r == 0, 32, 16)

    def swap_send(q):
        send(turned.at[1 - zl, :, pl.ds(START[q], CHUNKS[q])], sig[q].at[pl.ds(6 * y + 3 * zl, 3)],
             swap_s.at[q], swap_r.at[q], peer)

    def swap_wait(q):
        got(sig[q].at[pl.ds(6 * y + 3 * (1 - zl), 3)], swap_s.at[q], swap_r.at[q])

    def y_piece(q, yo, hr):
        h = zl if hr == 0 else 1 - zl
        return sig[q].at[pl.ds(6 * yo + 3 * h, 3)]

    def y_send(q, d, s, hr):
        sgn = 1 - 2 * d
        ref = y_piece(q, (y - sgn * (s - 1) + 8) % 8, hr)
        send(ref, ref, y_s.at[q, d, hr, s - 1], y_r.at[q, d, hr, s - 1], at(dy=sgn))

    def y_first(q, hr):
        for d in range(2):
            y_send(q, d, 1, hr)

    def y_step(q, s, hr):
        for d in range(2):
            last = 4 if d == hr else 3
            if s > last:
                continue
            sgn = 1 - 2 * d
            got(y_piece(q, (y - sgn * s + 8) % 8, hr), y_s.at[q, d, hr, s - 1], y_r.at[q, d, hr, s - 1])
            if s < last:
                y_send(q, d, s + 1, hr)

    def blk_copy(j):
        lo = 8 * j
        return copy(blk_hbm.at[pl.ds(lo, 8)], peer_blk.at[pl.ds(lo, 8)], blk_s.at[j], blk_r.at[j],
                    at(dz=1 if j % 2 == 0 else -1))

    def tab_make():
        tab_v[...] = jnp.zeros_like(tab_v)
        tab_v[0:1, 0:32] = pos[0]
        for i, v in enumerate(tables(tab_v[0:1], count[0, 0])):
            tab_v[i:i + 1] = v
        send(tab_v, peer_tab_v, tab_s.at[0], tab_r.at[0], peer)
        cp = pltpu.make_async_copy(tab_v, tab_own, loc.at[4])
        cp.start()
        cp.wait()

    def blk_send():
        for j in range(2):
            blk_copy(j).start()

        @pl.when(r == 0)
        def _():
            for j in range(2, 4):
                blk_copy(j).start()

    def blk_wait():
        for j in range(2):
            blk_copy(j).wait_recv()

        @pl.when(r == 0)
        def _():
            for j in range(2, 4):
                blk_copy(j).wait_recv()

    def blk_done():
        for j in range(2):
            blk_copy(j).wait_send()

        @pl.when(r == 0)
        def _():
            for j in range(2, 4):
                blk_copy(j).wait_send()

    def split_blocks(rel):
        src = own_blk if rel == 0 else peer_blk

        @pl.loop(0, n_slots)
        def _(i):
            hi, lo = split(src[i])
            blk_hi[rel, i] = hi
            blk_lo[rel, i] = lo

    def prep_own():
        local[0].wait()
        split_blocks(0)

    def prep_peer():
        got(peer_tab_v, tab_s.at[0], tab_r.at[0])
        cp = pltpu.make_async_copy(peer_tab_v, peer_tab, loc.at[3])
        cp.start()
        blk_wait()
        split_blocks(1)
        cp.wait()

    def prep_feat():
        local[1].wait()
        for i in range(3):
            for h in range(2):
                t = feat[i * BLK:(i + 1) * BLK, h * BLK:(h + 1) * BLK].T
                t = t.reshape(8, 2, 8, BLK)
                for kk in range(2):
                    hi, lo = split(t[:, kk].reshape(64, BLK))
                    row = kk * BLK + h * 64
                    ft_hi[row:row + 64, i * BLK:(i + 1) * BLK] = hi
                    ft_lo[row:row + 64, i * BLK:(i + 1) * BLK] = lo

    def prep_w():
        local[2].wait()
        for q in range(Q):
            lo, n = START[q], CHUNKS[q]
            v = jnp.concatenate([wv[:, zz * BLK + lo:zz * BLK + lo + n] for zz in range(8)], axis=1)
            w_hi[q][...], w_lo[q][...] = split(v)

    def spmm(q, rel):
        tab = tab_own if rel == 0 else peer_tab
        f = CHUNKS[q]

        def step(it, acc):
            terms = []
            for u in range(4):
                i = it * 4 + u
                sh, sl = split(sig[q][tab[0, i]])
                o = tab[1, i]
                t = dot(jnp.concatenate([sh, sl], axis=0), blk_hi[rel, o])
                t = t[:f] + t[f:] + dot(sh, blk_lo[rel, o])
                terms.append(t * tab[2, i].astype(F32))
            for u in range(4):
                i = it * 4 + u
                acc = terms[u] + acc * tab[3, i].astype(F32)
                run[i, 0:f] = acc
            return acc

        lax.fori_loop(0, n_slots // 4, step, jnp.zeros((f, BLK), F32))
        for b in range(24):
            rr = b // 3
            part[q][rr // 2, rr % 2, rel, b % 3] = run[tab[4, b], 0:f] * tab[5, b].astype(F32)

    def core_send(q, rel):
        for o in (2, 1, 3, 0):
            xx = (x + o) % 4
            send(part[q].at[xx, 1 - k, rel], core_in[q].at[xx, rel],
                 core_s.at[q, rel, o], core_r.at[q, rel, o], at(dk=1))

    def core_sum(q, rel, o):
        xx = (x + o) % 4
        got(core_in[q].at[xx, rel], core_s.at[q, rel, o], core_r.at[q, rel, o])
        part[q][xx, k, rel] = part[q][xx, k, rel] + core_in[q][xx, rel]

    def x_far(q, rel):
        core_sum(q, rel, 2)
        xx = (x + 2) % 4
        f = CHUNKS[q] // 2
        for h, sgn in ((0, 1), (1, -1)):
            send(part[q].at[xx, k, rel, :, pl.ds(h * f, f)], far_in[q].at[rel, h],
                 far_s.at[q, rel, h], far_r.at[q, rel, h], at(dx=sgn))

    def x_near(q, rel):
        f = CHUNKS[q] // 2
        for h, sgn in ((0, 1), (1, -1)):
            o = sgn % 4
            core_sum(q, rel, o)
            xx = (x + o) % 4
            got(far_in[q].at[rel, h], far_s.at[q, rel, h], far_r.at[q, rel, h])
            part[q][xx, k, rel, :, h * f:(h + 1) * f] = part[q][xx, k, rel, :, h * f:(h + 1) * f] + far_in[q][rel, h]
            send(part[q].at[xx, k, rel], near_in[q].at[rel, h],
                 near_s.at[q, rel, h], near_r.at[q, rel, h], at(dx=sgn))
        core_sum(q, rel, 0)

    def z_piece(q, dz):
        return back[q].at[pl.ds(((z + dz + 8) % 8) * CHUNKS[q], CHUNKS[q])]

    def z_half(q, dz, d):
        f = CHUNKS[q] // 2
        return back[q].at[pl.ds(((z + dz + 8) % 8) * 2 * f + d * f, f)]

    def z_start(q, rel):
        for h in range(2):
            got(near_in[q].at[rel, h], near_s.at[q, rel, h], near_r.at[q, rel, h])
        for i in range(3):
            v = part[q][x, k, rel, i] + near_in[q][rel, 0, i] + near_in[q][rel, 1, i]
            if rel == 0:
                back[q][pl.ds(z * CHUNKS[q], CHUNKS[q]), i * BLK:(i + 1) * BLK] = v
            else:
                other[q][:, i * BLK:(i + 1) * BLK] = v
        for d, sgn in ((0, 1), (1, -1)):
            if rel == 0:
                send(z_piece(q, 0), z_piece(q, 0), z_s.at[q, 2 + d], z_r.at[q, 2 + d], at(dz=2 * sgn))
            else:
                send(other[q], z_piece(q, 0), z_s.at[q, d], z_r.at[q, d], at(dz=sgn))

    def z_near(q):
        for d, sgn in ((0, 1), (1, -1)):
            ref = z_piece(q, -sgn)
            got(ref, z_s.at[q, d], z_r.at[q, d])
            send(ref, ref, z_s.at[q, 4 + d], z_r.at[q, 4 + d], at(dz=2 * sgn))

    def z_two(q):
        for d, sgn in ((0, 1), (1, -1)):
            got(z_piece(q, -2 * sgn), z_s.at[q, 2 + d], z_r.at[q, 2 + d])
            ref = z_half(q, -2 * sgn, d)
            send(ref, ref, z_s.at[q, 6 + d], z_r.at[q, 6 + d], at(dz=2 * sgn))

    def z_end(q):
        for d, sgn in ((0, 1), (1, -1)):
            got(z_piece(q, -3 * sgn), z_s.at[q, 4 + d], z_r.at[q, 4 + d])
        for d, sgn in ((0, 1), (1, -1)):
            got(z_half(q, -4 * sgn, d), z_s.at[q, 6 + d], z_r.at[q, 6 + d])

    def gw_dot(q):
        bh, bl = split(back[q][...])
        back_hi[q][...] = bh
        back_lo[q][...] = bl
        g = dot3(ft_hi[...], ft_lo[...], bh, bl, dot_nt)
        w = 2 * CHUNKS[q]
        for xx in range(4):
            v = g[:, xx * w:(xx + 1) * w].reshape(2, BLK, w)
            if w < BLK:
                v = jnp.concatenate([v[:, :64], v[:, 64:]], axis=2)
            gw[q][xx] = v
        gw_send(q)

    def gf(q):
        t = dot3(w_hi[q][...], w_lo[q][...], back_hi[q][...], back_lo[q][...], dot)
        if q > 0:
            t = gft[...] + t
        if q < Q - 1:
            gft[...] = t
        else:
            for i in range(3):
                for h in range(2):
                    gf_out[i * BLK:(i + 1) * BLK, h * BLK:(h + 1) * BLK] = (
                        t[h * BLK:(h + 1) * BLK, i * BLK:(i + 1) * BLK].T)

    def gw_row(q, j):
        rr = (r + j) % 8
        return copy(gw[q].at[rr // 2, rr % 2], gw_in[q].at[j], gwr_s.at[q, j], gwr_r.at[q, j],
                    {"row": rr, "col": c, "depth": zh})

    def gw_col(q, j):
        cc = (c + j) % 16
        return copy(gw_half[q].at[cc % (CHUNKS[q] // 4)], gw_yz[q].at[j], gwy_s.at[q, j], gwy_r.at[q, j],
                    {"row": r, "col": cc, "depth": zh})

    def gw_all(q, j):
        rr = (r + j) % 8
        return copy(gw_fin[q].at[r], gw_fin[q].at[r], gwf_s.at[q, j], gwf_r.at[q, j],
                    {"row": rr, "col": c, "depth": zh})

    def gw_all_in(q, j):
        ref = gw_fin[q].at[(r - j + 8) % 8]
        return copy(ref, ref, gwf_s.at[q, j], gwf_r.at[q, j], peer)

    def gw_send(q):
        @pl.loop(1, 8)
        def _(j):
            gw_row(q, j).start()

    def gw_sum(q):
        @pl.loop(1, 8)
        def _(j):
            gw_row(q, j).wait_recv()
        v = gw[q][x, k]
        for j in range(1, 8):
            v = v + gw_in[q][j]
        gw_half[q][...] = v.reshape(CHUNKS[q] // 4, 8, BLK)

        @pl.loop(1, 16)
        def _(j):
            gw_col(q, j).start()

    def gw_cols(q):
        @pl.loop(1, 16)
        def _(j):
            gw_col(q, j).wait_recv()
        v = gw_half[q][c % (CHUNKS[q] // 4)]
        for j in range(1, 16):
            v = v + gw_yz[q][j]
        if CHUNKS[q] == 32:
            v = jnp.concatenate([jnp.where(c < 8, v[:, :64], v[:, 64:])] * 2, axis=1)
        gw_fin[q][r] = v

        @pl.loop(1, 8)
        def _(j):
            gw_all(q, j).start()

    def gw_end():
        for q in range(Q):
            @pl.loop(1, 8)
            def _(j):
                gw_all_in(q, j).wait_recv()
        for zz in range(8):
            for kk in range(2):
                v = [gw_fin[q][(zz // 2) * 2 + kk][:, (zz % 2) * n:(zz % 2 + 1) * n] for q, n in enumerate(CHUNKS)]
                gw_out[kk * 8:(kk + 1) * 8, zz * BLK:(zz + 1) * BLK] = jnp.concatenate(v, axis=1)

    def drain():
        for cp in pending:
            cp.wait_send()
        blk_done()
        for q in range(Q):
            @pl.loop(1, 8)
            def _(j):
                gw_row(q, j).wait_send()
                gw_all(q, j).wait_send()

            @pl.loop(1, 16)
            def _(j):
                gw_col(q, j).wait_send()

    order = [
        (swap_send, 0), (swap_send, 1), (blk_send,), (y_first, 0, 0), (swap_wait, 0), (y_first, 0, 1),
        (y_step, 0, 1, 0), (prep_own,), (y_step, 0, 1, 1), (swap_wait, 1), (y_step, 0, 2, 0), (tab_make,),
        (y_step, 0, 2, 1), (prep_w,), (y_first, 1, 0), (y_step, 0, 3, 0), (y_step, 0, 3, 1), (y_first, 1, 1),
        (prep_feat,), (y_step, 1, 1, 0), (y_step, 0, 4, 1), (y_step, 0, 4, 0), (spmm, 0, 0), (y_step, 1, 1, 1),
        (core_send, 0, 0), (prep_peer,), (y_step, 1, 2, 0), (x_far, 0, 0), (spmm, 0, 1), (y_step, 1, 2, 1),
        (core_send, 0, 1), (x_near, 0, 0), (y_step, 1, 3, 0), (x_far, 0, 1), (y_step, 1, 3, 1), (z_start, 0, 0),
        (x_near, 0, 1), (y_step, 1, 4, 0), (y_step, 1, 4, 1), (spmm, 1, 0), (core_send, 1, 0), (z_start, 0, 1),
        (spmm, 1, 1), (core_send, 1, 1), (x_far, 1, 0), (z_near, 0), (x_far, 1, 1), (z_two, 0), (x_near, 1, 0),
        (x_near, 1, 1), (z_start, 1, 0), (z_start, 1, 1), (z_end, 0), (gw_dot, 0), (z_two, 1), (gf, 0),
        (z_near, 1), (gw_sum, 0), (z_end, 1), (gw_dot, 1), (gf, 1), (gw_cols, 0), (gw_sum, 1), (gw_cols, 1),
        (gw_end,), (drain,),
    ]
    for fn, *args in order:
        fn(*args)


def body(upstream, preact, features, weight, blocks, block_pos, block_count):
    vmem = pl.BlockSpec(memory_space=pltpu.VMEM)
    smem = pl.BlockSpec(memory_space=pltpu.SMEM)
    hbm = pl.BlockSpec(memory_space=pl.ANY)
    dma = pltpu.SemaphoreType.DMA
    V = pltpu.VMEM
    scratch = [
        V((2, 3, BLK, BLK), F32),
        V((8, BLK), jnp.int32), pltpu.SMEM((8, BLK), jnp.int32),
        V((8, BLK), jnp.int32), pltpu.SMEM((8, BLK), jnp.int32),
        V((32, BLK, BLK), F32), V((32, BLK, BLK), F32),
        V((2, 32, BLK, BLK), BF16), V((2, 32, BLK, BLK), BF16),
        V((32, max(CHUNKS), BLK), F32),
        V((384, 256), F32), V((256, 1024), F32),
        V((256, 384), BF16), V((256, 384), BF16),
        V((256, 384), F32),
    ]
    for shape, dtype in (
        (lambda f: (48, f, BLK), F32), (lambda f: (4, 2, 2, 3, f, BLK), F32), (lambda f: (4, 2, 3, f, BLK), F32),
        (lambda f: (2, 2, 3, f // 2, BLK), F32), (lambda f: (2, 2, 3, f, BLK), F32),
        (lambda f: (8 * f, 384), F32), (lambda f: (f, 384), F32),
        (lambda f: (8 * f, 384), BF16), (lambda f: (8 * f, 384), BF16),
        (lambda f: (256, 8 * f), BF16), (lambda f: (256, 8 * f), BF16),
        (lambda f: (4, 2, 2 * f, BLK), F32), (lambda f: (8, 2 * f, BLK), F32),
        (lambda f: (f // 4, 8, BLK), F32), (lambda f: (16, 8, BLK), F32), (lambda f: (8, 8, BLK), F32),
    ):
        scratch += [V(shape(f), dtype) for f in CHUNKS]
    scratch += [
        dma((5,)), dma((Q,)), dma((Q,)), dma((1,)), dma((1,)), dma((4,)), dma((4,)),
        dma((Q, 2, 2, 4)), dma((Q, 2, 2, 4)), dma((Q, 2, 4)), dma((Q, 2, 4)),
        dma((Q, 2, 2)), dma((Q, 2, 2)), dma((Q, 2, 2)), dma((Q, 2, 2)), dma((Q, 8)), dma((Q, 8)),
        dma((Q, 8)), dma((Q, 8)), dma((Q, 16)), dma((Q, 16)), dma((Q, 8)), dma((Q, 8)),
    ]
    return pl.pallas_call(
        kernel,
        out_shape=(jax.ShapeDtypeStruct((384, 256), F32), jax.ShapeDtypeStruct((16, 1024), F32)),
        in_specs=[vmem, vmem, vmem, smem, hbm, hbm, hbm],
        out_specs=(vmem, vmem),
        scratch_shapes=scratch,
        compiler_params=pltpu.CompilerParams(
            collective_id=0, has_side_effects=True, vmem_limit_bytes=56 * 2**20),
        cost_estimate=pl.CostEstimate(flops=2 * 10**9, bytes_accessed=6 * 2**20, transcendentals=0),
        name="graph_backward",
    )(upstream, preact, block_pos, block_count, features, weight, blocks.reshape(blocks.shape[2:]))


def solution(mesh):
    in_specs = (
        P(("row", "col"), "depth"),
        P(("row", "col"), "depth"),
        P(("col", "row"), "depth"),
        P("depth", None),
        P("row", "col", None, None, None),
        P("row", "col", None),
        P("row", "col"),
    )
    out_specs = (P(("col", "row"), "depth"), P(("depth", "col"), None))
    return jax.shard_map(body, mesh=mesh, in_specs=in_specs, out_specs=out_specs, check_vma=False)
```

time: 115 us -> 105 us (0.913)
  Pallas kernels: 109 us -> 100 us
  other arithmetic: 1.3 us -> 0 us
    pallas_call x1, Pallas kernels: 109 us -> 100 us  [body(): pl.pallas_call(kernel, out_shape=(jax.ShapeDtypeStruct((384, 256), F32),...]
where the time goes in v2:
time: 105 us
  Pallas kernels  100 us (95%)
  local copies, waits for them, and re-layouts  3.24 us (3%)
  between operations  1.29 us (1%)
    pallas_call x1, Pallas kernels, body(): pl.pallas_call(kernel, out_shape=(jax.ShapeDtypeStruct((384, 256), F32),...  100 us
    unnamed x2, local copies, waits for them, and re-layouts  3.24 us

profile of v2, /device:TPU:1, one launch (start us, length us, event | category | flops | bytes accessed | tf_op | source)
XLA Modules:
  0.0 104.5 jit_solution(13003702930657845181)
XLA Ops:
  1.3 100.0 %graph_backward.1 = (f32[384,256]{1,0:T(8,128)}, f32[16,1024]{1,0:T(8,128)}) custom-call(f32[384,256]{1,0:T(8,128)} %up.1, f32[384,256]{1,0:T(8,128)} %pre.1, s32[1,1,32]{2,1,0:T(1,128)} %pos.1, s32[1,1]{1,0:T(1,128)S(6)} %copy.11.count, f32[384,256]{1,0:T(8,128)} %feat_hbm.1, f32[256,1024]{1,0:T(8,128)} %w_hbm.1, f32[32,128,128]{2,1,0:T(8,128)} %bitcast.1), custom_call_target="tpu_custom_call" | custom-call | flops 2000000000 | bytes 6291456 | tf_op jit(solution)/shard_map/graph_backward/pallas_call | solution.py:482
  101.3 1.8 %copy.12 = f32[384,256]{1,0:T(8,128)} copy(f32[384,256]{1,0:T(8,128)} %get-tuple-element.4) | data formatting | bytes 786432
  103.0 1.5 %copy.13 = f32[16,1024]{1,0:T(8,128)} copy(f32[16,1024]{1,0:T(8,128)} %get-tuple-element.5) | data formatting | bytes 131072

commit v3 on v2

--- a/solution.py
+++ b/solution.py
@@ -6,7 +6,7 @@
 from jax.sharding import PartitionSpec as P
 
 BLK = 128
-CHUNKS = (64, 64)
+CHUNKS = (32, 32, 32, 32)
 Q = len(CHUNKS)
 START = tuple(sum(CHUNKS[:q]) for q in range(Q))
 MESH = pl.DeviceIdType.MESH
@@ -62,14 +62,15 @@
     return [put(down(brow)), put(ii), put(down(live)), put(down(cont)), last, has]
 
 
-def kernel(up, pre, pos, count, feat_hbm, w_hbm, blk_hbm, gf_out, gw_out,
-           turned, tab_v, tab_own, peer_tab_v, peer_tab, own_blk, peer_blk, blk_hi, blk_lo, run,
+def kernel(up_hbm, pre_hbm, pos, count, feat_hbm, w_hbm, blk_hbm, gf_hbm, gw_hbm,
+           up, pre, gf_out, gw_out, turned, tab_v, tab_own, peer_tab_v, peer_tab, own_blk, peer_blk, blk_hi, blk_lo, run,
            feat, wv, ft_hi, ft_lo, gft, *rest):
-    parts = [rest[i * Q:(i + 1) * Q] for i in range(16)]
-    (sig, part, core_in, far_in, near_in, back, other, back_hi, back_lo, w_hi, w_lo,
+    gwc, gwc_in, gwc_fin, *rest = rest
+    parts = [rest[i * Q:(i + 1) * Q] for i in range(15)]
+    (sig, part, core_in, near_in, back, other, back_hi, back_lo, w_hi, w_lo,
      gw, gw_in, gw_half, gw_yz, gw_fin) = parts
     (loc, swap_s, swap_r, tab_s, tab_r, blk_s, blk_r, y_s, y_r, core_s, core_r,
-     far_s, far_r, near_s, near_r, z_s, z_r, gwr_s, gwr_r, gwy_s, gwy_r, gwf_s, gwf_r) = rest[16 * Q:]
+     near_s, near_r, z_s, z_r, gwr_s, gwr_r, gwy_s, gwy_r, gwf_s, gwf_r) = rest[15 * Q:]
 
     r = lax.axis_index("row")
     c = lax.axis_index("col")
@@ -98,14 +99,17 @@
     def got(dst, ssem, rsem):
         copy(dst, dst, ssem, rsem, peer).wait_recv()
 
+    local = [pltpu.make_async_copy(s, d, loc.at[i]) for i, (s, d) in enumerate(
+        ((blk_hbm, own_blk), (feat_hbm, feat), (w_hbm, wv), (up_hbm, up), (pre_hbm, pre)))]
+    local[3].start()
+    local[4].start()
+
     bar = pltpu.get_barrier_semaphore()
-    for dev in (at(dx=1), at(dx=-1), at(dk=1), at(dy=1), at(dy=-1), at(dz=1), at(dz=-1), at(dz=2), at(dz=-2)):
+    for dev in (at(dx=2), at(dx=1), at(dx=-1), at(dk=1), at(dy=1), at(dy=-1), at(dz=1), at(dz=-1), at(dz=2), at(dz=-2)):
         pl.semaphore_signal(bar, inc=1, device_id=dev, device_id_type=MESH)
 
-    local = [pltpu.make_async_copy(s, d, loc.at[i]) for i, (s, d) in enumerate(
-        ((blk_hbm, own_blk), (feat_hbm, feat), (w_hbm, wv)))]
-    for cp in local:
-        cp.start()
+    local[3].wait()
+    local[4].wait()
 
     for i in range(3):
         for h in range(2):
@@ -117,7 +121,10 @@
         for q in range(Q):
             sig[q][6 * y + 3 * zl + i] = v[START[q]:START[q] + CHUNKS[q]]
 
-    pl.semaphore_wait(bar, 9)
+    for cp in local[:3]:
+        cp.start()
+
+    pl.semaphore_wait(bar, 10)
 
     n_slots = jnp.where(r == 0, 32, 16)
 
@@ -162,7 +169,7 @@
         for i, v in enumerate(tables(tab_v[0:1], count[0, 0])):
             tab_v[i:i + 1] = v
         send(tab_v, peer_tab_v, tab_s.at[0], tab_r.at[0], peer)
-        cp = pltpu.make_async_copy(tab_v, tab_own, loc.at[4])
+        cp = pltpu.make_async_copy(tab_v, tab_own, loc.at[5])
         cp.start()
         cp.wait()
 
@@ -268,24 +275,17 @@
         got(core_in[q].at[xx, rel], core_s.at[q, rel, o], core_r.at[q, rel, o])
         part[q][xx, k, rel] = part[q][xx, k, rel] + core_in[q][xx, rel]
 
+    def x_send(q, rel, o):
+        core_sum(q, rel, o)
+        send(part[q].at[(x + o) % 4, k, rel], near_in[q].at[rel, o - 1],
+             near_s.at[q, rel, o - 1], near_r.at[q, rel, o - 1], at(dx=o))
+
     def x_far(q, rel):
-        core_sum(q, rel, 2)
-        xx = (x + 2) % 4
-        f = CHUNKS[q] // 2
-        for h, sgn in ((0, 1), (1, -1)):
-            send(part[q].at[xx, k, rel, :, pl.ds(h * f, f)], far_in[q].at[rel, h],
-                 far_s.at[q, rel, h], far_r.at[q, rel, h], at(dx=sgn))
+        x_send(q, rel, 2)
 
     def x_near(q, rel):
-        f = CHUNKS[q] // 2
-        for h, sgn in ((0, 1), (1, -1)):
-            o = sgn % 4
-            core_sum(q, rel, o)
-            xx = (x + o) % 4
-            got(far_in[q].at[rel, h], far_s.at[q, rel, h], far_r.at[q, rel, h])
-            part[q][xx, k, rel, :, h * f:(h + 1) * f] = part[q][xx, k, rel, :, h * f:(h + 1) * f] + far_in[q][rel, h]
-            send(part[q].at[xx, k, rel], near_in[q].at[rel, h],
-                 near_s.at[q, rel, h], near_r.at[q, rel, h], at(dx=sgn))
+        x_send(q, rel, 1)
+        x_send(q, rel, 3)
         core_sum(q, rel, 0)
 
     def z_piece(q, dz):
@@ -296,10 +296,10 @@
         return back[q].at[pl.ds(((z + dz + 8) % 8) * 2 * f + d * f, f)]
 
     def z_start(q, rel):
-        for h in range(2):
+        for h in range(3):
             got(near_in[q].at[rel, h], near_s.at[q, rel, h], near_r.at[q, rel, h])
         for i in range(3):
-            v = part[q][x, k, rel, i] + near_in[q][rel, 0, i] + near_in[q][rel, 1, i]
+            v = (part[q][x, k, rel, i] + near_in[q][rel, 0, i]) + (near_in[q][rel, 1, i] + near_in[q][rel, 2, i])
             if rel == 0:
                 back[q][pl.ds(z * CHUNKS[q], CHUNKS[q]), i * BLK:(i + 1) * BLK] = v
             else:
@@ -333,6 +333,14 @@
         back_hi[q][...] = bh
         back_lo[q][...] = bl
         g = dot3(ft_hi[...], ft_lo[...], bh, bl, dot_nt)
+        if q == Q - 1:
+            for kk in range(2):
+                gwc[:, kk] = g[kk * BLK:(kk + 1) * BLK].reshape(16, 8, 8 * CHUNKS[q])
+
+            @pl.loop(0, 15)
+            def _(i):
+                gwc_col(far16(i)).start()
+            return
         w = 2 * CHUNKS[q]
         for xx in range(4):
             v = g[:, xx * w:(xx + 1) * w].reshape(2, BLK, w)
@@ -352,6 +360,13 @@
                 for h in range(2):
                     gf_out[i * BLK:(i + 1) * BLK, h * BLK:(h + 1) * BLK] = (
                         t[h * BLK:(h + 1) * BLK, i * BLK:(i + 1) * BLK].T)
+            pltpu.make_async_copy(gf_out, gf_hbm, loc.at[7]).start()
+
+    def far8(i):
+        return 4 + (1 - 2 * (i % 2)) * ((i + 1) // 2)
+
+    def far16(i):
+        return 8 + (1 - 2 * (i % 2)) * ((i + 1) // 2)
 
     def gw_row(q, j):
         rr = (r + j) % 8
@@ -365,17 +380,22 @@
 
     def gw_all(q, j):
         rr = (r + j) % 8
-        return copy(gw_fin[q].at[r], gw_fin[q].at[r], gwf_s.at[q, j], gwf_r.at[q, j],
-                    {"row": rr, "col": c, "depth": zh})
+        ref = (gwc_fin if q == Q - 1 else gw_fin[q]).at[r]
+        return copy(ref, ref, gwf_s.at[q, j], gwf_r.at[q, j], {"row": rr, "col": c, "depth": zh})
 
     def gw_all_in(q, j):
-        ref = gw_fin[q].at[(r - j + 8) % 8]
+        ref = (gwc_fin if q == Q - 1 else gw_fin[q]).at[(r - j + 8) % 8]
         return copy(ref, ref, gwf_s.at[q, j], gwf_r.at[q, j], peer)
 
+    def gwc_col(j):
+        cc = (c + j) % 16
+        return copy(gwc.at[cc], gwc_in.at[j], gwy_s.at[Q - 1, j], gwy_r.at[Q - 1, j],
+                    {"row": r, "col": cc, "depth": zh})
+
     def gw_send(q):
-        @pl.loop(1, 8)
-        def _(j):
-            gw_row(q, j).start()
+        @pl.loop(0, 7)
+        def _(i):
+            gw_row(q, far8(i)).start()
 
     def gw_sum(q):
         @pl.loop(1, 8)
@@ -386,61 +406,100 @@
             v = v + gw_in[q][j]
         gw_half[q][...] = v.reshape(CHUNKS[q] // 4, 8, BLK)
 
-        @pl.loop(1, 16)
-        def _(j):
-            gw_col(q, j).start()
+        @pl.loop(0, 15)
+        def _(i):
+            gw_col(q, far16(i)).start()
 
     def gw_cols(q):
-        @pl.loop(1, 16)
-        def _(j):
-            gw_col(q, j).wait_recv()
-        v = gw_half[q][c % (CHUNKS[q] // 4)]
-        for j in range(1, 16):
-            v = v + gw_yz[q][j]
-        if CHUNKS[q] == 32:
-            v = jnp.concatenate([jnp.where(c < 8, v[:, :64], v[:, 64:])] * 2, axis=1)
-        gw_fin[q][r] = v
-
+        if q == Q - 1:
+            @pl.loop(1, 16)
+            def _(j):
+                gwc_col(j).wait_recv()
+            v = gwc[c]
+            for j in range(1, 16):
+                v = v + gwc_in[j]
+            gwc_fin[r] = v
+        else:
+            @pl.loop(1, 16)
+            def _(j):
+                gw_col(q, j).wait_recv()
+            v = gw_half[q][c % (CHUNKS[q] // 4)]
+            for j in range(1, 16):
+                v = v + gw_yz[q][j]
+            if CHUNKS[q] == 32:
+                v = jnp.concatenate([jnp.where(c < 8, v[:, :64], v[:, 64:])] * 2, axis=1)
+            gw_fin[q][r] = v
+
+        @pl.loop(0, 7)
+        def _(i):
+            gw_all(q, far8(i)).start()
+
+    def gw_end(q):
         @pl.loop(1, 8)
         def _(j):
-            gw_all(q, j).start()
-
-    def gw_end():
+            gw_all_in(q, j).wait_recv()
+        n = CHUNKS[q]
+        for kk in range(2):
+            if q == Q - 1:
+                v = gwc_fin[0, kk]
+                for j in range(1, 8):
+                    v = v + gwc_fin[j, kk]
+            for zz in range(8):
+                if q == Q - 1:
+                    u = v[:, zz * n:(zz + 1) * n]
+                else:
+                    u = gw_fin[q][(zz // 2) * 2 + kk][:, (zz % 2) * n:(zz % 2 + 1) * n]
+                lane = zz * BLK + START[q]
+                gw_out[kk * 8:(kk + 1) * 8, lane:lane + n] = u
+
+    def early():
+        for cp in pending:
+            cp.wait_send()
+        pending.clear()
+        blk_done()
+        for q in range(Q - 1):
+            @pl.loop(1, 8)
+            def _(j):
+                gw_row(q, j).wait_send()
+
+    def drain():
+        last = pltpu.make_async_copy(gw_out, gw_hbm, loc.at[8])
+        last.start()
+        for cp in pending:
+            cp.wait_send()
         for q in range(Q):
             @pl.loop(1, 8)
             def _(j):
-                gw_all_in(q, j).wait_recv()
-        for zz in range(8):
-            for kk in range(2):
-                v = [gw_fin[q][(zz // 2) * 2 + kk][:, (zz % 2) * n:(zz % 2 + 1) * n] for q, n in enumerate(CHUNKS)]
-                gw_out[kk * 8:(kk + 1) * 8, zz * BLK:(zz + 1) * BLK] = jnp.concatenate(v, axis=1)
-
-    def drain():
-        for cp in pending:
-            cp.wait_send()
-        blk_done()
-        for q in range(Q):
-            @pl.loop(1, 8)
-            def _(j):
-                gw_row(q, j).wait_send()
                 gw_all(q, j).wait_send()
 
             @pl.loop(1, 16)
             def _(j):
-                gw_col(q, j).wait_send()
+                (gwc_col(j) if q == Q - 1 else gw_col(q, j)).wait_send()
+        pltpu.make_async_copy(gf_out, gf_hbm, loc.at[7]).wait()
+        last.wait()
 
     order = [
-        (swap_send, 0), (swap_send, 1), (blk_send,), (y_first, 0, 0), (swap_wait, 0), (y_first, 0, 1),
-        (y_step, 0, 1, 0), (prep_own,), (y_step, 0, 1, 1), (swap_wait, 1), (y_step, 0, 2, 0), (tab_make,),
-        (y_step, 0, 2, 1), (prep_w,), (y_first, 1, 0), (y_step, 0, 3, 0), (y_step, 0, 3, 1), (y_first, 1, 1),
-        (prep_feat,), (y_step, 1, 1, 0), (y_step, 0, 4, 1), (y_step, 0, 4, 0), (spmm, 0, 0), (y_step, 1, 1, 1),
-        (core_send, 0, 0), (prep_peer,), (y_step, 1, 2, 0), (x_far, 0, 0), (spmm, 0, 1), (y_step, 1, 2, 1),
-        (core_send, 0, 1), (x_near, 0, 0), (y_step, 1, 3, 0), (x_far, 0, 1), (y_step, 1, 3, 1), (z_start, 0, 0),
-        (x_near, 0, 1), (y_step, 1, 4, 0), (y_step, 1, 4, 1), (spmm, 1, 0), (core_send, 1, 0), (z_start, 0, 1),
-        (spmm, 1, 1), (core_send, 1, 1), (x_far, 1, 0), (z_near, 0), (x_far, 1, 1), (z_two, 0), (x_near, 1, 0),
-        (x_near, 1, 1), (z_start, 1, 0), (z_start, 1, 1), (z_end, 0), (gw_dot, 0), (z_two, 1), (gf, 0),
-        (z_near, 1), (gw_sum, 0), (z_end, 1), (gw_dot, 1), (gf, 1), (gw_cols, 0), (gw_sum, 1), (gw_cols, 1),
-        (gw_end,), (drain,),
+        (swap_send, 0), (swap_send, 1), (y_first, 0, 0), (swap_send, 2), (blk_send,), (prep_feat,), (prep_w,),
+        (swap_wait, 0), (y_first, 0, 1), (y_step, 0, 1, 0), (y_first, 1, 0), (swap_wait, 1), (swap_send, 3),
+        (y_first, 1, 1), (tab_make,), (swap_wait, 2), (prep_own,), (y_step, 0, 1, 1), (y_step, 0, 2, 0),
+        (y_step, 1, 1, 0), (y_step, 0, 2, 1), (y_step, 1, 1, 1), (y_first, 2, 0), (y_step, 0, 3, 0),
+        (y_step, 0, 3, 1), (y_step, 1, 2, 0), (y_first, 2, 1), (y_step, 1, 2, 1), (y_step, 2, 1, 0),
+        (y_step, 0, 4, 0), (y_step, 0, 4, 1), (spmm, 0, 0), (y_step, 1, 3, 0), (core_send, 0, 0),
+        (y_step, 2, 1, 1), (y_step, 1, 3, 1), (y_first, 3, 0), (x_far, 0, 0), (y_step, 2, 2, 0), (prep_peer,),
+        (spmm, 0, 1), (swap_wait, 3), (y_step, 2, 2, 1), (y_first, 3, 1), (core_send, 0, 1), (y_step, 1, 4, 1),
+        (x_near, 0, 0), (y_step, 1, 4, 0), (spmm, 1, 0), (y_step, 3, 1, 0), (x_far, 0, 1), (core_send, 1, 0),
+        (y_step, 2, 3, 1), (y_step, 2, 3, 0), (x_near, 0, 1), (y_step, 3, 1, 1), (z_start, 0, 0), (spmm, 1, 1),
+        (x_far, 1, 0), (y_step, 3, 2, 0), (x_near, 1, 0), (core_send, 1, 1), (z_start, 0, 1), (y_step, 2, 4, 0),
+        (y_step, 3, 2, 1), (y_step, 2, 4, 1), (spmm, 2, 0), (x_far, 1, 1), (y_step, 3, 3, 0), (x_near, 1, 1),
+        (z_start, 1, 0), (core_send, 2, 0), (z_near, 0), (y_step, 3, 3, 1), (spmm, 2, 1), (x_far, 2, 0),
+        (y_step, 3, 4, 0), (z_two, 0), (core_send, 2, 1), (x_near, 2, 0), (z_start, 1, 1), (y_step, 3, 4, 1),
+        (spmm, 3, 0), (core_send, 3, 0), (z_two, 1), (x_far, 2, 1), (x_near, 2, 1), (z_start, 2, 0),
+        (spmm, 3, 1), (x_far, 3, 0), (core_send, 3, 1), (z_near, 1), (x_near, 3, 0), (x_far, 3, 1),
+        (z_start, 2, 1), (z_end, 0), (x_near, 3, 1), (z_two, 2), (z_start, 3, 0), (gw_dot, 0), (z_start, 3, 1),
+        (z_end, 1), (z_near, 2), (gw_dot, 1), (z_two, 3), (gf, 0), (z_near, 3), (gf, 1), (gw_sum, 0),
+        (z_end, 2), (gw_dot, 2), (gw_sum, 1), (z_end, 3), (gw_dot, 3), (gf, 2), (early,), (gf, 3), (gw_sum, 2),
+        (gw_cols, 1), (gw_cols, 0), (gw_end, 1), (gw_cols, 3), (gw_cols, 2), (gw_end, 0), (gw_end, 3),
+        (gw_end, 2), (drain,),
     ]
     for fn, *args in order:
         fn(*args)
@@ -453,6 +512,8 @@
     dma = pltpu.SemaphoreType.DMA
     V = pltpu.VMEM
     scratch = [
+        V((384, 256), F32), V((384, 256), F32),
+        V((384, 256), F32), V((16, 1024), F32),
         V((2, 3, BLK, BLK), F32),
         V((8, BLK), jnp.int32), pltpu.SMEM((8, BLK), jnp.int32),
         V((8, BLK), jnp.int32), pltpu.SMEM((8, BLK), jnp.int32),
@@ -462,10 +523,11 @@
         V((384, 256), F32), V((256, 1024), F32),
         V((256, 384), BF16), V((256, 384), BF16),
         V((256, 384), F32),
+        V((16, 2, 8, 8 * CHUNKS[-1]), F32), V((16, 2, 8, 8 * CHUNKS[-1]), F32), V((8, 2, 8, 8 * CHUNKS[-1]), F32),
     ]
     for shape, dtype in (
         (lambda f: (48, f, BLK), F32), (lambda f: (4, 2, 2, 3, f, BLK), F32), (lambda f: (4, 2, 3, f, BLK), F32),
-        (lambda f: (2, 2, 3, f // 2, BLK), F32), (lambda f: (2, 2, 3, f, BLK), F32),
+        (lambda f: (2, 3, 3, f, BLK), F32),
         (lambda f: (8 * f, 384), F32), (lambda f: (f, 384), F32),
         (lambda f: (8 * f, 384), BF16), (lambda f: (8 * f, 384), BF16),
         (lambda f: (256, 8 * f), BF16), (lambda f: (256, 8 * f), BF16),
@@ -474,16 +536,16 @@
     ):
         scratch += [V(shape(f), dtype) for f in CHUNKS]
     scratch += [
-        dma((5,)), dma((Q,)), dma((Q,)), dma((1,)), dma((1,)), dma((4,)), dma((4,)),
+        dma((9,)), dma((Q,)), dma((Q,)), dma((1,)), dma((1,)), dma((4,)), dma((4,)),
         dma((Q, 2, 2, 4)), dma((Q, 2, 2, 4)), dma((Q, 2, 4)), dma((Q, 2, 4)),
-        dma((Q, 2, 2)), dma((Q, 2, 2)), dma((Q, 2, 2)), dma((Q, 2, 2)), dma((Q, 8)), dma((Q, 8)),
+        dma((Q, 2, 3)), dma((Q, 2, 3)), dma((Q, 8)), dma((Q, 8)),
         dma((Q, 8)), dma((Q, 8)), dma((Q, 16)), dma((Q, 16)), dma((Q, 8)), dma((Q, 8)),
     ]
     return pl.pallas_call(
         kernel,
         out_shape=(jax.ShapeDtypeStruct((384, 256), F32), jax.ShapeDtypeStruct((16, 1024), F32)),
-        in_specs=[vmem, vmem, vmem, smem, hbm, hbm, hbm],
-        out_specs=(vmem, vmem),
+        in_specs=[hbm, hbm, vmem, smem, hbm, hbm, hbm],
+        out_specs=(hbm, hbm),
         scratch_shapes=scratch,
         compiler_params=pltpu.CompilerParams(
             collective_id=0, has_side_effects=True, vmem_limit_bytes=56 * 2**20),

time: 105 us -> 100 us (0.952)
  Pallas kernels: 100 us -> 95.3 us
    pallas_call x1, Pallas kernels: 100 us -> 95.3 us  [body(): pl.pallas_call(kernel, out_shape=(jax.ShapeDtypeStruct((384, 256), F32),...]
where the time goes in v3:
time: 100 us; the launch traced here: 99.9 us
  Pallas kernels  95.3 us (95%)
  local copies, waits for them, and re-layouts  3.24 us (3%)
  between operations  1.29 us (1%)
    pallas_call x1, Pallas kernels, body(): pl.pallas_call(kernel, out_shape=(jax.ShapeDtypeStruct((384, 256), F32),...  95.3 us
    unnamed x2, local copies, waits for them, and re-layouts  3.24 us

profile of v3, /device:TPU:1, one launch (start us, length us, event | category | flops | bytes accessed | tf_op | source)
XLA Modules:
  0.0 99.9 jit_solution(10065032574397072178)
XLA Ops:
  1.3 95.3 %graph_backward.1 = (f32[384,256]{1,0:T(8,128)}, f32[16,1024]{1,0:T(8,128)}) custom-call(f32[384,256]{1,0:T(8,128)} %up_hbm.1, f32[384,256]{1,0:T(8,128)} %pre_hbm.1, s32[1,1,32]{2,1,0:T(1,128)} %pos.1, s32[1,1]{1,0:T(1,128)S(6)} %copy.11.count, f32[384,256]{1,0:T(8,128)} %feat_hbm.1, f32[256,1024]{1,0:T(8,128)} %w_hbm.1, f32[32,128,128]{2,1,0:T(8,128)} %bitcast.1), custom_call_target="tpu_custom_call" | custom-call | flops 2000000000 | bytes 6291456 | tf_op jit(solution)/shard_map/graph_backward/pallas_call | solution.py:544
  96.6 1.8 %copy.12 = f32[384,256]{1,0:T(8,128)} copy(f32[384,256]{1,0:T(8,128)} %get-tuple-element.4) | data formatting | bytes 786432
  98.4 1.5 %copy.13 = f32[16,1024]{1,0:T(8,128)} copy(f32[16,1024]{1,0:T(8,128)} %get-tuple-element.5) | data formatting | bytes 131072

commit v4 on v3

--- a/solution.py
+++ b/solution.py
@@ -65,12 +65,12 @@
 def kernel(up_hbm, pre_hbm, pos, count, feat_hbm, w_hbm, blk_hbm, gf_hbm, gw_hbm,
            up, pre, gf_out, gw_out, turned, tab_v, tab_own, peer_tab_v, peer_tab, own_blk, peer_blk, blk_hi, blk_lo, run,
            feat, wv, ft_hi, ft_lo, gft, *rest):
-    gwc, gwc_in, gwc_fin, *rest = rest
-    parts = [rest[i * Q:(i + 1) * Q] for i in range(15)]
+    gwc, gwc_in, gwc_fin, gw_half, gw_yz, gw_fin, *rest = rest
+    parts = [rest[i * Q:(i + 1) * Q] for i in range(12)]
     (sig, part, core_in, near_in, back, other, back_hi, back_lo, w_hi, w_lo,
-     gw, gw_in, gw_half, gw_yz, gw_fin) = parts
+     gw, gw_in) = parts
     (loc, swap_s, swap_r, tab_s, tab_r, blk_s, blk_r, y_s, y_r, core_s, core_r,
-     near_s, near_r, z_s, z_r, gwr_s, gwr_r, gwy_s, gwy_r, gwf_s, gwf_r) = rest[15 * Q:]
+     near_s, near_r, z_s, z_r, gwr_s, gwr_r, gwy_s, gwy_r, gwf_s, gwf_r) = rest[12 * Q:]
 
     r = lax.axis_index("row")
     c = lax.axis_index("col")
@@ -337,9 +337,8 @@
             for kk in range(2):
                 gwc[:, kk] = g[kk * BLK:(kk + 1) * BLK].reshape(16, 8, 8 * CHUNKS[q])
 
-            @pl.loop(0, 15)
-            def _(i):
-                gwc_col(far16(i)).start()
+            for i in range(15):
+                gw_col(1, far16(i)).start()
             return
         w = 2 * CHUNKS[q]
         for xx in range(4):
@@ -356,10 +355,7 @@
         if q < Q - 1:
             gft[...] = t
         else:
-            for i in range(3):
-                for h in range(2):
-                    gf_out[i * BLK:(i + 1) * BLK, h * BLK:(h + 1) * BLK] = (
-                        t[h * BLK:(h + 1) * BLK, i * BLK:(i + 1) * BLK].T)
+            gf_out[...] = t
             pltpu.make_async_copy(gf_out, gf_hbm, loc.at[7]).start()
 
     def far8(i):
@@ -370,27 +366,31 @@
 
     def gw_row(q, j):
         rr = (r + j) % 8
-        return copy(gw[q].at[rr // 2, rr % 2], gw_in[q].at[j], gwr_s.at[q, j], gwr_r.at[q, j],
+        return copy(gw[q].at[rr // 2, rr % 2], gw_in[q].at[j], gwr_s.at[q], gwr_r.at[q],
                     {"row": rr, "col": c, "depth": zh})
 
-    def gw_col(q, j):
+    def gw_rows(q):
+        ref = gw_in[q].at[pl.ds(1, 7)]
+        return copy(ref, ref, gwr_s.at[q], gwr_r.at[q], peer)
+
+    src, inc, fin = (gw_half, gwc), (gw_yz, gwc_in), (gw_fin, gwc_fin)
+
+    def gw_col(g, j):
         cc = (c + j) % 16
-        return copy(gw_half[q].at[cc % (CHUNKS[q] // 4)], gw_yz[q].at[j], gwy_s.at[q, j], gwy_r.at[q, j],
+        return copy(src[g].at[cc if g else cc % 8], inc[g].at[j], gwy_s.at[g], gwy_r.at[g],
                     {"row": r, "col": cc, "depth": zh})
 
-    def gw_all(q, j):
-        rr = (r + j) % 8
-        ref = (gwc_fin if q == Q - 1 else gw_fin[q]).at[r]
-        return copy(ref, ref, gwf_s.at[q, j], gwf_r.at[q, j], {"row": rr, "col": c, "depth": zh})
-
-    def gw_all_in(q, j):
-        ref = (gwc_fin if q == Q - 1 else gw_fin[q]).at[(r - j + 8) % 8]
-        return copy(ref, ref, gwf_s.at[q, j], gwf_r.at[q, j], peer)
-
-    def gwc_col(j):
-        cc = (c + j) % 16
-        return copy(gwc.at[cc], gwc_in.at[j], gwy_s.at[Q - 1, j], gwy_r.at[Q - 1, j],
-                    {"row": r, "col": cc, "depth": zh})
+    def gw_all(g, j):
+        return copy(fin[g].at[0], fin[g].at[j], gwf_s.at[g], gwf_r.at[g],
+                    {"row": (r + j) % 8, "col": c, "depth": zh})
+
+    def gw_col_wait(g):
+        ref = inc[g].at[pl.ds(1, 15)]
+        return copy(ref, ref, gwy_s.at[g], gwy_r.at[g], peer)
+
+    def gw_all_wait(g):
+        ref = fin[g].at[pl.ds(1, 7)]
+        return copy(ref, ref, gwf_s.at[g], gwf_r.at[g], peer)
 
     def gw_send(q):
         @pl.loop(0, 7)
@@ -398,59 +398,47 @@
             gw_row(q, far8(i)).start()
 
     def gw_sum(q):
-        @pl.loop(1, 8)
-        def _(j):
-            gw_row(q, j).wait_recv()
+        gw_rows(q).wait_recv()
         v = gw[q][x, k]
         for j in range(1, 8):
             v = v + gw_in[q][j]
-        gw_half[q][...] = v.reshape(CHUNKS[q] // 4, 8, BLK)
-
-        @pl.loop(0, 15)
-        def _(i):
-            gw_col(q, far16(i)).start()
-
-    def gw_cols(q):
-        if q == Q - 1:
-            @pl.loop(1, 16)
-            def _(j):
-                gwc_col(j).wait_recv()
-            v = gwc[c]
-            for j in range(1, 16):
-                v = v + gwc_in[j]
-            gwc_fin[r] = v
-        else:
-            @pl.loop(1, 16)
-            def _(j):
-                gw_col(q, j).wait_recv()
-            v = gw_half[q][c % (CHUNKS[q] // 4)]
-            for j in range(1, 16):
-                v = v + gw_yz[q][j]
-            if CHUNKS[q] == 32:
-                v = jnp.concatenate([jnp.where(c < 8, v[:, :64], v[:, 64:])] * 2, axis=1)
-            gw_fin[q][r] = v
+        gw_half[:, q] = v.reshape(8, 8, BLK)
+        if q == Q - 2:
+            @pl.loop(0, 15)
+            def _(i):
+                gw_col(0, far16(i)).start()
+
+    def gw_cols(g):
+        gw_col_wait(g).wait_recv()
+        v = src[g][c if g else c % 8]
+        for j in range(1, 16):
+            v = v + inc[g][j]
+        if g == 0:
+            v = jnp.concatenate([jnp.where(c < 8, v[..., :64], v[..., 64:])] * 2, axis=2)
+        fin[g][0] = v
 
         @pl.loop(0, 7)
         def _(i):
-            gw_all(q, far8(i)).start()
-
-    def gw_end(q):
-        @pl.loop(1, 8)
-        def _(j):
-            gw_all_in(q, j).wait_recv()
-        n = CHUNKS[q]
-        for kk in range(2):
-            if q == Q - 1:
-                v = gwc_fin[0, kk]
-                for j in range(1, 8):
-                    v = v + gwc_fin[j, kk]
-            for zz in range(8):
-                if q == Q - 1:
-                    u = v[:, zz * n:(zz + 1) * n]
-                else:
-                    u = gw_fin[q][(zz // 2) * 2 + kk][:, (zz % 2) * n:(zz % 2 + 1) * n]
-                lane = zz * BLK + START[q]
-                gw_out[kk * 8:(kk + 1) * 8, lane:lane + n] = u
+            gw_all(g, far8(i)).start()
+
+    def gw_end(g):
+        gw_all_wait(g).wait_recv()
+        if g == 0:
+            for rr in range(8):
+                v = fin[0][(r - rr + 8) % 8]
+                for q in range(Q - 1):
+                    for zz in range(2):
+                        lane = (rr // 2 * 2 + zz) * BLK + START[q]
+                        gw_out[rr % 2 * 8:rr % 2 * 8 + 8, lane:lane + 32] = v[q, :, zz * 32:(zz + 1) * 32]
+        else:
+            v = fin[1][r]
+            for rr in range(1, 8):
+                v = v + fin[1][(r - rr + 8) % 8]
+            n = CHUNKS[-1]
+            for kk in range(2):
+                for zz in range(8):
+                    lane = zz * BLK + START[-1]
+                    gw_out[kk * 8:(kk + 1) * 8, lane:lane + n] = v[kk, :, zz * n:(zz + 1) * n]
 
     def early():
         for cp in pending:
@@ -458,51 +446,61 @@
         pending.clear()
         blk_done()
         for q in range(Q - 1):
-            @pl.loop(1, 8)
-            def _(j):
-                gw_row(q, j).wait_send()
+            gw_rows(q).wait_send()
 
     def drain():
         last = pltpu.make_async_copy(gw_out, gw_hbm, loc.at[8])
         last.start()
         for cp in pending:
             cp.wait_send()
-        for q in range(Q):
-            @pl.loop(1, 8)
-            def _(j):
-                gw_all(q, j).wait_send()
-
-            @pl.loop(1, 16)
-            def _(j):
-                (gwc_col(j) if q == Q - 1 else gw_col(q, j)).wait_send()
+        for g in range(2):
+            gw_col_wait(g).wait_send()
+            gw_all_wait(g).wait_send()
         pltpu.make_async_copy(gf_out, gf_hbm, loc.at[7]).wait()
         last.wait()
 
     order = [
-        (swap_send, 0), (swap_send, 1), (y_first, 0, 0), (swap_send, 2), (blk_send,), (prep_feat,), (prep_w,),
-        (swap_wait, 0), (y_first, 0, 1), (y_step, 0, 1, 0), (y_first, 1, 0), (swap_wait, 1), (swap_send, 3),
-        (y_first, 1, 1), (tab_make,), (swap_wait, 2), (prep_own,), (y_step, 0, 1, 1), (y_step, 0, 2, 0),
-        (y_step, 1, 1, 0), (y_step, 0, 2, 1), (y_step, 1, 1, 1), (y_first, 2, 0), (y_step, 0, 3, 0),
-        (y_step, 0, 3, 1), (y_step, 1, 2, 0), (y_first, 2, 1), (y_step, 1, 2, 1), (y_step, 2, 1, 0),
-        (y_step, 0, 4, 0), (y_step, 0, 4, 1), (spmm, 0, 0), (y_step, 1, 3, 0), (core_send, 0, 0),
-        (y_step, 2, 1, 1), (y_step, 1, 3, 1), (y_first, 3, 0), (x_far, 0, 0), (y_step, 2, 2, 0), (prep_peer,),
-        (spmm, 0, 1), (swap_wait, 3), (y_step, 2, 2, 1), (y_first, 3, 1), (core_send, 0, 1), (y_step, 1, 4, 1),
-        (x_near, 0, 0), (y_step, 1, 4, 0), (spmm, 1, 0), (y_step, 3, 1, 0), (x_far, 0, 1), (core_send, 1, 0),
-        (y_step, 2, 3, 1), (y_step, 2, 3, 0), (x_near, 0, 1), (y_step, 3, 1, 1), (z_start, 0, 0), (spmm, 1, 1),
-        (x_far, 1, 0), (y_step, 3, 2, 0), (x_near, 1, 0), (core_send, 1, 1), (z_start, 0, 1), (y_step, 2, 4, 0),
-        (y_step, 3, 2, 1), (y_step, 2, 4, 1), (spmm, 2, 0), (x_far, 1, 1), (y_step, 3, 3, 0), (x_near, 1, 1),
-        (z_start, 1, 0), (core_send, 2, 0), (z_near, 0), (y_step, 3, 3, 1), (spmm, 2, 1), (x_far, 2, 0),
-        (y_step, 3, 4, 0), (z_two, 0), (core_send, 2, 1), (x_near, 2, 0), (z_start, 1, 1), (y_step, 3, 4, 1),
-        (spmm, 3, 0), (core_send, 3, 0), (z_two, 1), (x_far, 2, 1), (x_near, 2, 1), (z_start, 2, 0),
-        (spmm, 3, 1), (x_far, 3, 0), (core_send, 3, 1), (z_near, 1), (x_near, 3, 0), (x_far, 3, 1),
-        (z_start, 2, 1), (z_end, 0), (x_near, 3, 1), (z_two, 2), (z_start, 3, 0), (gw_dot, 0), (z_start, 3, 1),
-        (z_end, 1), (z_near, 2), (gw_dot, 1), (z_two, 3), (gf, 0), (z_near, 3), (gf, 1), (gw_sum, 0),
-        (z_end, 2), (gw_dot, 2), (gw_sum, 1), (z_end, 3), (gw_dot, 3), (gf, 2), (early,), (gf, 3), (gw_sum, 2),
-        (gw_cols, 1), (gw_cols, 0), (gw_end, 1), (gw_cols, 3), (gw_cols, 2), (gw_end, 0), (gw_end, 3),
-        (gw_end, 2), (drain,),
+        (swap_send, 0), (y_first, 0, 0), (swap_send, 1), (swap_send, 2), (swap_send, 3), (blk_send,),
+        (swap_wait, 0), (y_first, 0, 1), (y_first, 1, 0), (swap_wait, 1), (swap_wait, 2), (y_first, 1, 1),
+        (tab_make,), (y_step, 0, 1, 0), (swap_wait, 3), (prep_w,), (y_step, 0, 1, 1), (y_step, 1, 1, 0),
+        (y_step, 1, 1, 1), (y_step, 0, 2, 0), (prep_own,), (y_step, 0, 2, 1), (y_step, 1, 2, 0),
+        (y_step, 1, 2, 1), (y_first, 2, 0), (y_step, 0, 3, 1), (y_step, 0, 3, 0), (y_first, 2, 1),
+        (y_step, 1, 3, 0), (y_step, 1, 3, 1), (y_step, 2, 1, 0), (y_step, 0, 4, 1), (y_step, 0, 4, 0),
+        (y_first, 3, 0), (spmm, 0, 0), (core_send, 0, 0), (y_step, 2, 1, 1), (y_first, 3, 1), (y_step, 1, 4, 0),
+        (y_step, 1, 4, 1), (spmm, 1, 0), (y_step, 2, 2, 0), (core_send, 1, 0), (prep_peer,), (x_far, 0, 0),
+        (y_step, 3, 1, 0), (spmm, 1, 1), (y_step, 2, 2, 1), (x_near, 0, 0), (core_send, 1, 1),
+        (y_step, 3, 1, 1), (x_far, 1, 0), (spmm, 0, 1), (x_near, 1, 0), (y_step, 3, 2, 0), (y_step, 2, 3, 0),
+        (core_send, 0, 1), (x_far, 1, 1), (y_step, 2, 3, 1), (z_start, 0, 0), (x_near, 1, 1), (x_far, 0, 1),
+        (y_step, 3, 2, 1), (prep_feat,), (y_step, 3, 3, 0), (z_start, 1, 0), (x_near, 0, 1), (y_step, 2, 4, 0),
+        (y_step, 2, 4, 1), (spmm, 2, 0), (core_send, 2, 0), (z_start, 1, 1), (y_step, 3, 3, 1), (z_two, 0),
+        (spmm, 2, 1), (x_far, 2, 0), (y_step, 3, 4, 0), (z_start, 0, 1), (x_near, 2, 0), (z_two, 1),
+        (core_send, 2, 1), (z_near, 1), (y_step, 3, 4, 1), (spmm, 3, 0), (core_send, 3, 0), (x_far, 2, 1),
+        (spmm, 3, 1), (z_start, 2, 0), (x_near, 2, 1), (z_near, 0), (x_far, 3, 0), (core_send, 3, 1),
+        (x_near, 3, 0), (x_far, 3, 1), (z_start, 2, 1), (x_near, 3, 1), (z_two, 2), (z_start, 3, 0),
+        (z_start, 3, 1), (z_end, 0), (z_end, 1), (z_near, 2), (gw_dot, 0), (gf, 0), (z_two, 3), (z_near, 3),
+        (gw_dot, 1), (z_end, 2), (gw_dot, 2), (gf, 1), (z_end, 3), (gw_dot, 3), (gw_sum, 0), (gw_sum, 1),
+        (gf, 2), (early,), (gf, 3), (gw_sum, 2), (gw_cols, 1), (gw_cols, 0), (gw_end, 1), (gw_end, 0), (drain,),
     ]
     for fn, *args in order:
         fn(*args)
+
+
+def finish(gft_hbm, gw_hbm, gf_out, gw_out, gft, gf, gw, sem):
+    a = pltpu.make_async_copy(gft_hbm, gft, sem.at[0])
+    b = pltpu.make_async_copy(gw_hbm, gw, sem.at[1])
+    a.start()
+    b.start()
+    a.wait()
+    for i in range(3):
+        for h in range(2):
+            gf[i * BLK:(i + 1) * BLK, h * BLK:(h + 1) * BLK] = gft[h * BLK:(h + 1) * BLK, i * BLK:(i + 1) * BLK].T
+    c = pltpu.make_async_copy(gf, gf_out, sem.at[2])
+    c.start()
+    b.wait()
+    d = pltpu.make_async_copy(gw, gw_out, sem.at[3])
+    d.start()
+    c.wait()
+    d.wait()
 
 
 def body(upstream, preact, features, weight, blocks, block_pos, block_count):
@@ -513,7 +511,7 @@
     V = pltpu.VMEM
     scratch = [
         V((384, 256), F32), V((384, 256), F32),
-        V((384, 256), F32), V((16, 1024), F32),
+        V((256, 384), F32), V((16, 1024), F32),
         V((2, 3, BLK, BLK), F32),
         V((8, BLK), jnp.int32), pltpu.SMEM((8, BLK), jnp.int32),
         V((8, BLK), jnp.int32), pltpu.SMEM((8, BLK), jnp.int32),
@@ -524,6 +522,7 @@
         V((256, 384), BF16), V((256, 384), BF16),
         V((256, 384), F32),
         V((16, 2, 8, 8 * CHUNKS[-1]), F32), V((16, 2, 8, 8 * CHUNKS[-1]), F32), V((8, 2, 8, 8 * CHUNKS[-1]), F32),
+        V((8, Q - 1, 8, BLK), F32), V((16, Q - 1, 8, BLK), F32), V((8, Q - 1, 8, BLK), F32),
     ]
     for shape, dtype in (
         (lambda f: (48, f, BLK), F32), (lambda f: (4, 2, 2, 3, f, BLK), F32), (lambda f: (4, 2, 3, f, BLK), F32),
@@ -532,18 +531,17 @@
         (lambda f: (8 * f, 384), BF16), (lambda f: (8 * f, 384), BF16),
         (lambda f: (256, 8 * f), BF16), (lambda f: (256, 8 * f), BF16),
         (lambda f: (4, 2, 2 * f, BLK), F32), (lambda f: (8, 2 * f, BLK), F32),
-        (lambda f: (f // 4, 8, BLK), F32), (lambda f: (16, 8, BLK), F32), (lambda f: (8, 8, BLK), F32),
     ):
         scratch += [V(shape(f), dtype) for f in CHUNKS]
     scratch += [
         dma((9,)), dma((Q,)), dma((Q,)), dma((1,)), dma((1,)), dma((4,)), dma((4,)),
         dma((Q, 2, 2, 4)), dma((Q, 2, 2, 4)), dma((Q, 2, 4)), dma((Q, 2, 4)),
         dma((Q, 2, 3)), dma((Q, 2, 3)), dma((Q, 8)), dma((Q, 8)),
-        dma((Q, 8)), dma((Q, 8)), dma((Q, 16)), dma((Q, 16)), dma((Q, 8)), dma((Q, 8)),
+        dma((Q,)), dma((Q,)), dma((2,)), dma((2,)), dma((2,)), dma((2,)),
     ]
-    return pl.pallas_call(
+    turned_gf, gw = pl.pallas_call(
         kernel,
-        out_shape=(jax.ShapeDtypeStruct((384, 256), F32), jax.ShapeDtypeStruct((16, 1024), F32)),
+        out_shape=(jax.ShapeDtypeStruct((256, 384), F32), jax.ShapeDtypeStruct((16, 1024), F32)),
         in_specs=[hbm, hbm, vmem, smem, hbm, hbm, hbm],
         out_specs=(hbm, hbm),
         scratch_shapes=scratch,
@@ -552,6 +550,14 @@
         cost_estimate=pl.CostEstimate(flops=2 * 10**9, bytes_accessed=6 * 2**20, transcendentals=0),
         name="graph_backward",
     )(upstream, preact, block_pos, block_count, features, weight, blocks.reshape(blocks.shape[2:]))
+    return pl.pallas_call(
+        finish,
+        out_shape=(jax.ShapeDtypeStruct((384, 256), F32), jax.ShapeDtypeStruct((16, 1024), F32)),
+        in_specs=[hbm, hbm], out_specs=(hbm, hbm),
+        scratch_shapes=[V((256, 384), F32), V((384, 256), F32), V((16, 1024), F32), dma((4,))],
+        compiler_params=pltpu.CompilerParams(vmem_limit_bytes=56 * 2**20),
+        name="finish",
+    )(turned_gf, gw)
 
 
 def solution(mesh):

time: 100 us -> 97 us (0.970)
  local copies, waits for them, and re-layouts: 3.24 us -> 0 us
    unnamed x2 -> x0, local copies, waits for them, and re-layouts: 3.24 us -> none
    pallas_call x1 -> x2, Pallas kernels: 95.3 us -> 95.5 us  [the longest x1 93.5 us: body(): pl.pallas_call(kernel, out_shape=(jax.ShapeDtypeStruct((256, 384), F32),...]
where the time goes in v4:
time: 97 us; the launch traced here: 96.8 us
  Pallas kernels  95.5 us (98%)
  between operations  1.29 us (1%)
    pallas_call x1, Pallas kernels, body(): pl.pallas_call(kernel, out_shape=(jax.ShapeDtypeStruct((256, 384), F32),...  93.5 us
    pallas_call x1, Pallas kernels, body(): pl.pallas_call(finish, out_shape=(jax.ShapeDtypeStruct((384, 256), F32),...  1.96 us

profile of v4, /device:TPU:1, one launch (start us, length us, event | category | flops | bytes accessed | tf_op | source)
XLA Modules:
  0.0 96.8 jit_solution(16371065982913517093)
XLA Ops:
  1.3 93.5 %graph_backward.1 = (f32[256,384]{1,0:T(8,128)}, f32[16,1024]{1,0:T(8,128)}) custom-call(f32[384,256]{1,0:T(8,128)} %up_hbm.1, f32[384,256]{1,0:T(8,128)} %pre_hbm.1, s32[1,1,32]{2,1,0:T(1,128)} %pos.1, s32[1,1]{1,0:T(1,128)S(6)} %copy.9.count, f32[384,256]{1,0:T(8,128)} %feat_hbm.1, f32[256,1024]{1,0:T(8,128)} %w_hbm.1, f32[32,128,128]{2,1,0:T(8,128)} %bitcast.1), custom_call_target="tpu_custom_call" | custom-call | flops 2000000000 | bytes 6291456 | tf_op jit(solution)/shard_map/graph_backward/pallas_call | solution.py:542
  94.8 2.0 %finish.1 = (f32[384,256]{1,0:T(8,128)}, f32[16,1024]{1,0:T(8,128)}) custom-call(f32[256,384]{1,0:T(8,128)} %get-tuple-element.4.gft_hbm, f32[16,1024]{1,0:T(8,128)} %get-tuple-element.5.gw_hbm), custom_call_target="tpu_custom_call" | custom-call | tf_op jit(solution)/shard_map/finish/pallas_call | solution.py:553

commit v5 on v4

--- a/solution.py
+++ b/solution.py
@@ -404,8 +404,7 @@
             v = v + gw_in[q][j]
         gw_half[:, q] = v.reshape(8, 8, BLK)
         if q == Q - 2:
-            @pl.loop(0, 15)
-            def _(i):
+            for i in range(15):
                 gw_col(0, far16(i)).start()
 
     def gw_cols(g):
@@ -417,8 +416,7 @@
             v = jnp.concatenate([jnp.where(c < 8, v[..., :64], v[..., 64:])] * 2, axis=2)
         fin[g][0] = v
 
-        @pl.loop(0, 7)
-        def _(i):
+        for i in range(7):
             gw_all(g, far8(i)).start()
 
     def gw_end(g):
@@ -460,47 +458,49 @@
         last.wait()
 
     order = [
-        (swap_send, 0), (y_first, 0, 0), (swap_send, 1), (swap_send, 2), (swap_send, 3), (blk_send,),
-        (swap_wait, 0), (y_first, 0, 1), (y_first, 1, 0), (swap_wait, 1), (swap_wait, 2), (y_first, 1, 1),
-        (tab_make,), (y_step, 0, 1, 0), (swap_wait, 3), (prep_w,), (y_step, 0, 1, 1), (y_step, 1, 1, 0),
-        (y_step, 1, 1, 1), (y_step, 0, 2, 0), (prep_own,), (y_step, 0, 2, 1), (y_step, 1, 2, 0),
-        (y_step, 1, 2, 1), (y_first, 2, 0), (y_step, 0, 3, 1), (y_step, 0, 3, 0), (y_first, 2, 1),
-        (y_step, 1, 3, 0), (y_step, 1, 3, 1), (y_step, 2, 1, 0), (y_step, 0, 4, 1), (y_step, 0, 4, 0),
-        (y_first, 3, 0), (spmm, 0, 0), (core_send, 0, 0), (y_step, 2, 1, 1), (y_first, 3, 1), (y_step, 1, 4, 0),
-        (y_step, 1, 4, 1), (spmm, 1, 0), (y_step, 2, 2, 0), (core_send, 1, 0), (prep_peer,), (x_far, 0, 0),
-        (y_step, 3, 1, 0), (spmm, 1, 1), (y_step, 2, 2, 1), (x_near, 0, 0), (core_send, 1, 1),
-        (y_step, 3, 1, 1), (x_far, 1, 0), (spmm, 0, 1), (x_near, 1, 0), (y_step, 3, 2, 0), (y_step, 2, 3, 0),
-        (core_send, 0, 1), (x_far, 1, 1), (y_step, 2, 3, 1), (z_start, 0, 0), (x_near, 1, 1), (x_far, 0, 1),
-        (y_step, 3, 2, 1), (prep_feat,), (y_step, 3, 3, 0), (z_start, 1, 0), (x_near, 0, 1), (y_step, 2, 4, 0),
-        (y_step, 2, 4, 1), (spmm, 2, 0), (core_send, 2, 0), (z_start, 1, 1), (y_step, 3, 3, 1), (z_two, 0),
-        (spmm, 2, 1), (x_far, 2, 0), (y_step, 3, 4, 0), (z_start, 0, 1), (x_near, 2, 0), (z_two, 1),
-        (core_send, 2, 1), (z_near, 1), (y_step, 3, 4, 1), (spmm, 3, 0), (core_send, 3, 0), (x_far, 2, 1),
-        (spmm, 3, 1), (z_start, 2, 0), (x_near, 2, 1), (z_near, 0), (x_far, 3, 0), (core_send, 3, 1),
-        (x_near, 3, 0), (x_far, 3, 1), (z_start, 2, 1), (x_near, 3, 1), (z_two, 2), (z_start, 3, 0),
-        (z_start, 3, 1), (z_end, 0), (z_end, 1), (z_near, 2), (gw_dot, 0), (gf, 0), (z_two, 3), (z_near, 3),
-        (gw_dot, 1), (z_end, 2), (gw_dot, 2), (gf, 1), (z_end, 3), (gw_dot, 3), (gw_sum, 0), (gw_sum, 1),
-        (gf, 2), (early,), (gf, 3), (gw_sum, 2), (gw_cols, 1), (gw_cols, 0), (gw_end, 1), (gw_end, 0), (drain,),
+        (swap_send, 0), (swap_send, 1), (y_first, 0, 0), (swap_send, 2), (swap_send, 3), (blk_send,),
+        (swap_wait, 0), (y_first, 0, 1), (prep_own,), (tab_make,), (swap_wait, 1), (y_first, 1, 0),
+        (y_step, 0, 1, 0), (y_first, 1, 1), (swap_wait, 2), (y_step, 0, 1, 1), (swap_wait, 3), (y_first, 2, 0),
+        (y_step, 1, 1, 0), (y_step, 0, 2, 0), (y_step, 0, 2, 1), (prep_feat,), (y_step, 1, 1, 1),
+        (y_first, 2, 1), (y_step, 0, 3, 0), (y_step, 0, 3, 1), (prep_w,), (y_step, 1, 2, 1), (y_step, 1, 2, 0),
+        (y_step, 2, 1, 0), (y_step, 2, 1, 1), (y_step, 0, 4, 0), (y_step, 0, 4, 1), (spmm, 0, 0),
+        (core_send, 0, 0), (y_step, 1, 3, 1), (y_first, 3, 0), (y_step, 1, 3, 0), (x_far, 0, 0),
+        (y_first, 3, 1), (y_step, 2, 2, 0), (x_near, 0, 0), (prep_peer,), (y_step, 2, 2, 1), (spmm, 0, 1),
+        (core_send, 0, 1), (y_step, 1, 4, 1), (y_step, 3, 1, 0), (y_step, 1, 4, 0), (spmm, 1, 1),
+        (y_step, 3, 1, 1), (x_far, 0, 1), (z_start, 0, 0), (core_send, 1, 1), (x_near, 0, 1), (y_step, 2, 3, 0),
+        (y_step, 2, 3, 1), (spmm, 1, 0), (x_far, 1, 1), (y_step, 3, 2, 0), (core_send, 1, 0), (x_near, 1, 1),
+        (y_step, 3, 2, 1), (z_start, 0, 1), (y_step, 2, 4, 0), (x_far, 1, 0), (y_step, 2, 4, 1), (z_two, 0),
+        (spmm, 2, 0), (y_step, 3, 3, 0), (x_near, 1, 0), (core_send, 2, 0), (y_step, 3, 3, 1), (z_start, 1, 1),
+        (z_near, 0), (spmm, 2, 1), (core_send, 2, 1), (x_far, 2, 0), (y_step, 3, 4, 0), (x_near, 2, 0),
+        (z_start, 1, 0), (y_step, 3, 4, 1), (spmm, 3, 0), (core_send, 3, 0), (x_far, 2, 1), (z_near, 1),
+        (x_near, 2, 1), (spmm, 3, 1), (x_far, 3, 0), (core_send, 3, 1), (z_start, 2, 0), (x_near, 3, 0),
+        (z_end, 0), (x_far, 3, 1), (z_two, 1), (z_start, 2, 1), (x_near, 3, 1), (z_start, 3, 0), (gw_dot, 0),
+        (z_start, 3, 1), (gf, 0), (z_end, 1), (z_two, 2), (z_near, 2), (gw_dot, 1), (z_two, 3), (gf, 1),
+        (z_near, 3), (gw_sum, 0), (gw_sum, 1), (z_end, 2), (gw_dot, 2), (gf, 2), (z_end, 3), (gw_dot, 3),
+        (gf, 3), (early,), (gw_sum, 2), (gw_cols, 1), (gw_cols, 0), (gw_end, 1), (gw_end, 0), (drain,),
     ]
     for fn, *args in order:
         fn(*args)
 
 
 def finish(gft_hbm, gw_hbm, gf_out, gw_out, gft, gf, gw, sem):
-    a = pltpu.make_async_copy(gft_hbm, gft, sem.at[0])
-    b = pltpu.make_async_copy(gw_hbm, gw, sem.at[1])
-    a.start()
-    b.start()
-    a.wait()
+    into = [pltpu.make_async_copy(gft_hbm.at[:, pl.ds(i * BLK, BLK)], gft.at[:, pl.ds(i * BLK, BLK)], sem.at[i])
+            for i in range(3)]
+    into.append(pltpu.make_async_copy(gw_hbm, gw, sem.at[3]))
+    out = [pltpu.make_async_copy(gf.at[pl.ds(i * BLK, BLK)], gf_out.at[pl.ds(i * BLK, BLK)], sem.at[4 + i])
+           for i in range(3)]
+    out.append(pltpu.make_async_copy(gw, gw_out, sem.at[7]))
+    for cp in into:
+        cp.start()
     for i in range(3):
+        into[i].wait()
         for h in range(2):
             gf[i * BLK:(i + 1) * BLK, h * BLK:(h + 1) * BLK] = gft[h * BLK:(h + 1) * BLK, i * BLK:(i + 1) * BLK].T
-    c = pltpu.make_async_copy(gf, gf_out, sem.at[2])
-    c.start()
-    b.wait()
-    d = pltpu.make_async_copy(gw, gw_out, sem.at[3])
-    d.start()
-    c.wait()
-    d.wait()
+        out[i].start()
+    into[3].wait()
+    out[3].start()
+    for cp in out:
+        cp.wait()
 
 
 def body(upstream, preact, features, weight, blocks, block_pos, block_count):
@@ -554,7 +554,7 @@
         finish,
         out_shape=(jax.ShapeDtypeStruct((384, 256), F32), jax.ShapeDtypeStruct((16, 1024), F32)),
         in_specs=[hbm, hbm], out_specs=(hbm, hbm),
-        scratch_shapes=[V((256, 384), F32), V((384, 256), F32), V((16, 1024), F32), dma((4,))],
+        scratch_shapes=[V((256, 384), F32), V((384, 256), F32), V((16, 1024), F32), dma((8,))],
         compiler_params=pltpu.CompilerParams(vmem_limit_bytes=56 * 2**20),
         name="finish",
     )(turned_gf, gw)

time: 97 us -> 97.5 us (level)
  no operation moved by 1% of the time
where the time goes in v5:
time: 97.5 us; the launch traced here: 97.3 us
  Pallas kernels  96 us (98%)
  between operations  1.29 us (1%)
    pallas_call x1, Pallas kernels, body(): pl.pallas_call(kernel, out_shape=(jax.ShapeDtypeStruct((256, 384), F32),...  94.1 us
    pallas_call x1, Pallas kernels, body(): pl.pallas_call(finish, out_shape=(jax.ShapeDtypeStruct((384, 256), F32),...  1.95 us

profile of v5, /device:TPU:1, one launch (start us, length us, event | category | flops | bytes accessed | tf_op | source)
XLA Modules:
  0.0 97.3 jit_solution(14661243916864741581)
XLA Ops:
  1.3 94.1 %graph_backward.1 = (f32[256,384]{1,0:T(8,128)}, f32[16,1024]{1,0:T(8,128)}) custom-call(f32[384,256]{1,0:T(8,128)} %up_hbm.1, f32[384,256]{1,0:T(8,128)} %pre_hbm.1, s32[1,1,32]{2,1,0:T(1,128)} %pos.1, s32[1,1]{1,0:T(1,128)S(6)} %copy.9.count, f32[384,256]{1,0:T(8,128)} %feat_hbm.1, f32[256,1024]{1,0:T(8,128)} %w_hbm.1, f32[32,128,128]{2,1,0:T(8,128)} %bitcast.1), custom_call_target="tpu_custom_call" | custom-call | flops 2000000000 | bytes 6291456 | tf_op jit(solution)/shard_map/graph_backward/pallas_call | solution.py:542
  95.4 2.0 %finish.1 = (f32[384,256]{1,0:T(8,128)}, f32[16,1024]{1,0:T(8,128)}) custom-call(f32[256,384]{1,0:T(8,128)} %get-tuple-element.4.gft_hbm, f32[16,1024]{1,0:T(8,128)} %get-tuple-element.5.gw_hbm), custom_call_target="tpu_custom_call" | custom-call | tf_op jit(solution)/shard_map/finish/pallas_call | solution.py:553
